TPU v7x, 32 devices: a whole 2x2x4 slice. The times are simulated.
32 devices in a mesh: head: 1, blk: 32 (over z, y, x, core).
Axes of the slice: x: 2, y: 2, z: 4, core: 2. Of those that a mesh axis runs over, the one named last changes fastest.
Arguments:
- vision: bfloat16 [4, 1408, 2048], P(None, 'head', 'blk'), may hold values from -600 to 600
- ln_gain: float32 [1408], P('head'), may hold values from 0.5 to 1.5
- merge_proj: bfloat16 [4, 1408, 1408], P(None, 'head'), may hold values from -0.078125 to 0.078125
- image_slot: int32 [512], P('blk'), may hold values from 0 to 16380, as said below
- text: bfloat16 [1408, 16384], P('head', 'blk'), may hold values from -600 to 600
- rms_gain: float32 [1408], replicated, may hold values from 0.5 to 1.5
- wqkv: bfloat16 [3, 1408, 1408], P(None, 'head'), may hold values from -0.31835938 to 0.31835938
- pcache: bfloat16 [2, 1408, 65536], P(None, 'head', 'blk'), may hold values from -300 to 300
- block_table: int32 [32, 128], replicated, may hold values from -1 to 2047, as said below
- cache_len: int32 [32], P('blk'), may hold values from 1 to 4096, as said below
Outputs:
- attended: bfloat16 [1408, 16384], P('head', 'blk')
- new_cache: bfloat16 [2, 1408, 16384], P(None, 'head', 'blk')
Inputs may be any that keep to these rules, and one draw needn't show every extreme that they name: `image_slot`: pieces never intersect and start at multiples of 4; the 16 pieces held by one index of blk start in the rows of 16 different requests, and every request receives exactly 16 pieces. `block_table`: row r holds a block number for j < ceil(cache_len[r] / 32) and -1 after; no block number appears twice; index d of blk holds blocks d * 64 to (d+1) * 64 - 1. The longest request has exactly 4 blocks on every index of blk; every other request has at most one block on any index. `cache_len`: exactly one request, the longest, has 4096 cached positions; all others have fewer.
All inputs are finite; a program needn't handle non-finite values.
Results may differ from a plain program's by a relative error of at most 0.025.
The roundings to bfloat16 on the way count: a program that leaves them out, or rounds other values in their place, can miss the bound.
Values may be sent and summed in bfloat16 or wider, within the bound.
No kernel may reach another device: no remote copies, remote signals or barrier semaphores. Data moves between devices by JAX's collectives and lax.ppermute only.
A program may use at most 320 MiB of HBM per device.

v0:
```python
import math

import jax
import jax.numpy as jnp
from jax import lax
from jax.sharding import PartitionSpec as P

D = 1408
HD = 88
BS = 32


masked_score = -1e30


def rotary_columns(values, places):
    half = values.shape[1] // 2
    freq_index = jnp.arange(half, dtype=jnp.float32)
    inverse = jnp.exp(freq_index * (-2.0 * math.log(10000.0) / values.shape[1]))
    angles = inverse[:, None] * places[None, :]
    cosine = jnp.cos(angles)[None]
    sine_part = jnp.sin(angles)[None]
    leading = values[:, :half]
    trailing = values[:, half:]
    return jnp.concatenate(
        [leading * cosine - trailing * sine_part, trailing * cosine + leading * sine_part], axis=1
    )


def softmax_part(query_block, keys, values, mask, scale):
    scores = (
        jnp.einsum("hdq,hdk->hqk", query_block, keys, preferred_element_type=jnp.float32) * scale
    )
    scores = jnp.where(mask[None], scores, masked_score)
    highest = jnp.max(scores, axis=2)
    expo = jnp.where(mask[None], jnp.exp(scores - highest[:, :, None]), 0.0)
    total = jnp.sum(expo, axis=2)
    mixed = jnp.einsum("hqk,hdk->hdq", expo, values, precision=lax.Precision.HIGHEST)
    return (mixed, highest, total)


def fold_softmax(first, second):
    mixed_a, high_a, total_a = first
    mixed_b, high_b, total_b = second
    top = jnp.maximum(high_a, high_b)
    factor_a = jnp.exp(high_a - top)
    factor_b = jnp.exp(high_b - top)
    return (
        mixed_a * factor_a[:, None, :] + mixed_b * factor_b[:, None, :],
        top,
        total_a * factor_a + total_b * factor_b,
    )


def unblock(parts):
    mixed, highest, total = parts
    heads_here = mixed.shape[1]
    mixed = jnp.transpose(mixed, (1, 2, 0, 3)).reshape(heads_here, mixed.shape[2], -1)
    highest = jnp.transpose(highest, (1, 0, 2)).reshape(heads_here, -1)
    total = jnp.transpose(total, (1, 0, 2)).reshape(heads_here, -1)
    return (mixed, highest, total)


def shards(
    vision, ln_gain, merge_proj, image_slot, text, rms_gain, wqkv, pcache, block_table, cache_len
):
    local = vision.shape[1]
    groups = vision.shape[2]
    floats = vision.astype(jnp.float32)
    totals, squares = lax.psum((jnp.sum(floats, axis=1), jnp.sum(floats * floats, axis=1)), "head")
    average = totals / D
    spread = squares / D - average * average
    normed_vision = (
        (floats - average[:, None, :])
        * lax.rsqrt(spread + 1e-06)[:, None, :]
        * ln_gain[None, :, None]
    ).astype(jnp.bfloat16)
    partial_rows = jnp.einsum(
        "tcd,tcg->dg", merge_proj, normed_vision, preferred_element_type=jnp.float32
    )
    merged_columns = lax.psum_scatter(partial_rows, "head", scatter_dimension=0, tiled=True).astype(
        jnp.bfloat16
    )
    merged = jnp.transpose(merged_columns)
    devices = lax.axis_size("blk")
    here = lax.axis_index("blk")
    rows_here = text.shape[1]
    pieces = image_slot.shape[0]
    piece_rows = groups // pieces
    lines = jnp.arange(rows_here, dtype=jnp.int32)
    offsets = jnp.arange(piece_rows, dtype=jnp.int32)
    target = image_slot // rows_here
    within = image_slot % rows_here
    select = target[None, :] == jnp.arange(devices, dtype=jnp.int32)[:, None]
    outbound = (
        jnp.dot(
            select.astype(jnp.bfloat16),
            merged.reshape(pieces, piece_rows * local),
            preferred_element_type=jnp.float32,
        )
        .astype(jnp.bfloat16)
        .reshape(devices, piece_rows, local)
    )
    starts = jnp.sum(jnp.where(select, within[None, :] + 1, 0), axis=1) - 1
    arrived, arrived_start = (
        lax.all_to_all(outbound, "blk", split_axis=0, concat_axis=0, tiled=True),
        lax.all_to_all(starts, "blk", split_axis=0, concat_axis=0, tiled=True),
    )
    row_ids = (arrived_start[:, None] + offsets[None, :]).reshape(-1)
    present = jnp.repeat(arrived_start >= 0, piece_rows)
    hits = (row_ids[:, None] == lines[None, :]) & present[:, None]
    placed_rows = jnp.einsum(
        "kl,kr->lr",
        arrived.reshape(devices * piece_rows, local),
        hits.astype(jnp.bfloat16),
        preferred_element_type=jnp.float32,
    ).astype(jnp.bfloat16)
    covered = jnp.any(hits, axis=0)
    placed = jnp.where(covered[None, :], placed_rows, text)
    row_floats = placed.astype(jnp.float32)
    square_sums = lax.psum(jnp.sum(row_floats * row_floats, axis=0), "head")
    gain_here = lax.dynamic_slice_in_dim(rms_gain, lax.axis_index("head") * local, local)
    normed = (row_floats * lax.rsqrt(square_sums / D + 1e-06)[None, :] * gain_here[:, None]).astype(
        jnp.bfloat16
    )
    projected = jnp.einsum(
        "jod,dr->jor",
        wqkv,
        lax.all_gather(normed, "head", axis=0, tiled=True),
        preferred_element_type=jnp.float32,
    )
    heads_here = local // HD
    projected = projected.reshape(3, heads_here, HD, rows_here)
    places = (cache_len[0] + lines).astype(jnp.float32)
    queries = rotary_columns(projected[0], places).astype(jnp.bfloat16)
    new_keys = rotary_columns(projected[1], places).astype(jnp.bfloat16)
    new_values = projected[2].astype(jnp.bfloat16)
    new_cache = jnp.stack(
        [new_keys.reshape(local, rows_here), new_values.reshape(local, rows_here)], axis=0
    )
    block_len = BS
    owned = pcache.shape[2] // block_len
    paged = pcache.reshape(2, local, owned, block_len)
    requests = block_table.shape[0]
    table_width = block_table.shape[1]
    slots_each = table_width // devices
    block_ids = here * owned + jnp.arange(owned, dtype=jnp.int32)
    matches = block_table[None, :, :] == block_ids[:, None, None]
    found = jnp.any(matches, axis=2)
    in_use = jnp.any(found, axis=1)
    owner = jnp.sum(jnp.where(found, jnp.arange(requests, dtype=jnp.int32)[None, :], 0), axis=1)
    logical = jnp.sum(
        jnp.where(matches, jnp.arange(table_width, dtype=jnp.int32)[None, None, :], 0), axis=(1, 2)
    )
    counter = jnp.arange(owned, dtype=jnp.int32)
    earlier = (
        (owner[:, None] == owner[None, :]) & in_use[None, :] & (counter[None, :] < counter[:, None])
    )
    standing = jnp.sum(earlier.astype(jnp.int32), axis=1)
    within_block = jnp.arange(block_len, dtype=jnp.int32)
    block_rows = min(rows_here, 512)
    count_blocks = rows_here // block_rows
    scale = HD ** (-0.5)
    query_blocks = jnp.transpose(
        queries.reshape(heads_here, HD, count_blocks, block_rows), (2, 0, 1, 3)
    )
    first_rows = jnp.arange(count_blocks, dtype=jnp.int32) * block_rows
    destination = owner * slots_each + standing
    routing = (destination[None, :] == jnp.arange(table_width, dtype=jnp.int32)[:, None]) & in_use[
        None, :
    ]
    outgoing = jnp.einsum(
        "wo,cfob->cfwb", routing.astype(jnp.bfloat16), paged, preferred_element_type=jnp.float32
    ).astype(jnp.bfloat16)
    outgoing = outgoing.reshape(2, local, table_width * block_len)
    labels = jnp.sum(jnp.where(routing, logical[None, :] + 1, 0), axis=1) - 1
    labels = labels.reshape(1, 1, table_width)
    blocks_in, labels_in = (
        lax.all_to_all(outgoing, "blk", split_axis=2, concat_axis=2, tiled=True),
        lax.all_to_all(labels, "blk", split_axis=2, concat_axis=2, tiled=True),
    )
    cached_keys = blocks_in[0].reshape(heads_here, HD, -1)
    cached_values = blocks_in[1].reshape(heads_here, HD, -1).astype(jnp.float32)
    label_flat = labels_in.reshape(-1)
    key_places = label_flat[:, None] * block_len + within_block[None, :]
    live = ((label_flat[:, None] >= 0) & (key_places < cache_len[0])).reshape(-1)
    old_mask = jnp.broadcast_to(live[None, :], (block_rows, live.shape[0]))
    new_values_f = new_values.astype(jnp.float32)

    def attend(inputs):
        query_block, first_row = inputs
        causal = (first_row + jnp.arange(block_rows, dtype=jnp.int32))[:, None] >= lines[None, :]
        old_part = softmax_part(query_block, cached_keys, cached_values, old_mask, scale)
        own_part = softmax_part(query_block, new_keys, new_values_f, causal, scale)
        return fold_softmax(old_part, own_part)

    mixed, highest, total = unblock(lax.map(attend, (query_blocks, first_rows)))
    attended = (mixed / total[:, None, :]).astype(jnp.bfloat16).reshape(local, rows_here)
    return (attended, new_cache)


def solution(mesh):
    in_specs = (
        P(None, "head", "blk"),
        P("head"),
        P(None, "head", None),
        P("blk"),
        P("head", "blk"),
        P(),
        P(None, "head", None),
        P(None, "head", "blk"),
        P(),
        P("blk"),
    )
    out_specs = (P("head", "blk"), P(None, "head", "blk"))
    return jax.shard_map(shards, mesh=mesh, in_specs=in_specs, out_specs=out_specs, check_vma=False)
```

profile of v0, /device:TPU:0, one launch (start us, length us, event | category | flops | bytes accessed | tf_op | source)
XLA Modules:
  0.0 994.2 jit_solution(17669111374985458964)
XLA Ops:
  0.6 0.7 fusion.53
  1.4 0.7 copy.71
  2.1 7.3 all-to-all-start.2
  9.4 2.0 fusion.31
  11.4 3.1 compare_reduce_fusion
  14.5 1.4 convert_reduce_fusion
  16.0 0.2 convert_reduce_fusion.1
  16.4 8.6 fusion.22
  25.0 0.7 copy.70
  25.7 0.1 reshape.279
  25.9 5.8 all-to-all-start.1
  31.7 0.4 convolution_convert_fusion.1
  32.1 0.8 reshape.280
  32.9 15.5 %copy.65 = bf16[2,1408,2048]{1,2,0:T(8,128)(2,1)} copy(bf16[2,1408,2048]{2,1,0:T(8,128)(2,1)} %param.17) | data formatting | bytes 23068672 | tf_op args[7]
  48.4 5.8 all-to-all-start.3
  54.3 11.2 %fusion.8 = bf16[2,1408,128,32]{1,2,3,0:T(8,128)(2,1)S(1)} fusion(bf16[2,1408,64,32]{1,3,2,0:T(8,128)(2,1)} %bitcast.42, s32[64]{0:T(128)S(1)} %get-tuple-element.69, pred[64]{0:T(512)(128)(4,1)S(1)} %get-tuple-element.44), kind=kOutput, calls=%fused_computation.11 | convolution fusion | flops 1487945728 | bytes 34603328 | tf_op jit(solution)/shard_map/wo,cfob->cfwb/dot_general | solution.py:172
  65.5 15.5 %copy.67 = bf16[2,1408,128,32]{1,3,2,0:T(8,128)(2,1)} copy(bf16[2,1408,128,32]{1,2,3,0:T(8,128)(2,1)S(1)} %fusion.8) | data formatting | bytes 46137344 | tf_op jit(solution)/shard_map/convert_element_type | solution.py:174
  81.0 42.1 %copy.68 = bf16[2,1408,4096]{1,0,2:T(2,128)(2,1)} copy(bf16[2,1408,4096]{1,2,0:T(8,128)(2,1)} %bitcast.41) | data formatting | bytes 46137344 | tf_op jit(solution)/shard_map/reshape | solution.py:175
  123.2 6.1 all-to-all-start
  130.1 0.4 multiply_cosine_fusion
  130.5 0.7 reduce.3
  131.3 0.1 and.66
  131.6 0.1 fusion.40
  131.7 2.4 multiply_reduce_fusion
  134.1 2.4 compare_reduce_fusion.2
  136.7 0.7 fusion.18
  137.5 14.3 %convolution_bitcast_fusion = f32[3,1408,512]{1,2,0:T(8,128)} fusion(bf16[3,1408,1408]{2,1,0:T(8,128)(2,1)} %param.16, bf16[1408,512]{1,0:T(8,128)(2,1)S(1)} %get-tuple-element.64, f32[1408]{0:T(1024)S(1)} %copy-done.4, f32[512]{0:T(512)S(1)} %add_rsqrt_fusion), kind=kOutput, calls=%fused_computation.24 | convolution fusion | flops 6093012992 | bytes 21995008 | tf_op jit(solution)/shard_map/jod,dr->jor/dot_general | solution.py:126
  151.8 2.0 slice.57
  153.7 5.6 fusion.65
  159.3 3.4 copy.73
  162.7 1.5 copy.76
  164.3 3.4 copy.75
  167.7 2.4 multiply_subtract_fusion
  170.1 0.3 maximum_convert_fusion
  170.4 1.5 copy.78
  171.9 3.2 pad_maximum_fusion
  175.1 4.7 copy.79
  179.8 2.4 subtract_convert_fusion
  182.2 3.8 fusion.9
  186.0 4.0 fusion.10
  190.1 11.3 %fusion.11 = f32[16,88,512]{2,1,0:T(8,128)} fusion(bf16[16,88,512]{2,1,0:T(8,128)(2,1)S(1)} %bitcast.48, f32[16,512,512]{1,2,0:T(8,128)S(1)} %get-tuple-element.66, f32[16,512]{1,0:T(8,128)S(1)} %get-tuple-element.65, pred[512,512]{0,1:T(8,128)(4,1)S(1)} %iota_compare_fusion), kind=kOutput, calls=%fused_computation.16 | convolution fusion | flops 4445962240 | bytes 21397504 | tf_op jit(solution)/shard_map/while/body/eval_jaxpr/hqk,hdk->hdq/dot_general | solution.py:38
  201.3 441.7 %all-to-all-done = bf16[2,1408,4096]{1,0,2:T(2,128)(2,1)} async-done(((bf16[2,1408,4096]{1,0,2:T(2,128)(2,1)}), bf16[2,1408,4096]{1,0,2:T(2,128)(2,1)}, u32[]{:S(2)}, u32[]{:S(2)}) %all-to-all-start) | async-done | bytes 23068704 | tf_op jit(solution)/shard_map/all_to_all | solution.py:179
  643.1 44.3 %fusion.64 = (bf16[1,1408,4096]{1,0,2:T(2,128)(2,1)}, bf16[1,1408,4096]{1,0,2:T(2,128)(2,1)}) fusion(bf16[2,1408,4096]{1,0,2:T(2,128)(2,1)} %all-to-all-done), kind=kLoop, calls=%fused_computation.118 | loop fusion | bytes 46137344 | tf_op jit(solution)/shard_map/slice | solution.py:182
  687.4 48.7 %copy.74 = bf16[1,1408,4096]{2,1,0:T(8,128)(2,1)} copy(bf16[1,1408,4096]{1,0,2:T(2,128)(2,1)} %get-tuple-element.49) | data formatting | bytes 23068672 | tf_op jit(solution)/shard_map/slice | solution.py:182
  736.1 48.8 %copy.69 = bf16[1,1408,4096]{2,1,0:T(8,128)(2,1)} copy(bf16[1,1408,4096]{1,0,2:T(2,128)(2,1)} %get-tuple-element.50) | data formatting | bytes 23068672 | tf_op jit(solution)/shard_map/slice | solution.py:183
  784.9 49.6 %fusion = (f32[16,512]{1,0:T(8,128)S(1)}, f32[16,512,4096]{2,1,0:T(8,128)}) fusion(pred[4096]{0:T(1024)(128)(4,1)S(1)} %and.63, bf16[16,88,4096]{2,1,0:T(8,128)(2,1)} %bitcast.43, bf16[16,44,512]{2,1,0:T(8,128)(2,1)S(1)} %copy-done.1, bf16[16,44,512]{2,1,0:T(8,128)(2,1)S(1)} %get-tuple-element.53), kind=kOutput, calls=%fused_computation.2 | convolution fusion | flops 6009118720 | bytes 147230720 | tf_op jit(solution)/shard_map/while/body/eval_jaxpr/hdq,hdk->hqk/dot_general | solution.py:32
  834.6 41.5 %fusion.1 = f32[16,512]{1,0:T(8,128)S(1)} fusion(f32[16,512,4096]{2,1,0:T(8,128)} %get-tuple-element.68, f32[16,512]{1,0:T(8,128)S(1)} %get-tuple-element.67, pred[4096]{0:T(1024)(128)(4,1)S(1)} %and.63), kind=kLoop, calls=%fused_computation.3 | loop fusion | flops 167763968 | bytes 134287360 | tf_op jit(solution)/shard_map/while/body/eval_jaxpr/reduce_sum | solution.py:37
  876.1 117.6 %divide_convert_fusion = bf16[16,88,512]{2,1,0:T(8,128)(2,1)} fusion(f32[16,88,512]{2,1,0:T(8,128)} %fusion.11, bf16[16,88,4096]{2,1,0:T(8,128)(2,1)} %bitcast.47, f32[16,512,4096]{2,1,0:T(8,128)} %get-tuple-element.68, f32[16,512]{1,0:T(8,128)S(1)} %get-tuple-element.67, pred[4096]{0:T(1024)(128)(4,1)S(1)} %and.63, f32[16,512]{1,0:T(8,128)S(1)} %get-tuple-element.46, ...), kind=kOutput, calls=%fused_computation.34 | convolution fusion | flops 35571302400 | bytes 150212608 | tf_op jit(solution)/shard_map/while/body/eval_jaxpr/hqk,hdk->hdq/dot_general | solution.py:38
  (33 shorter events, 1.0 us)
Async XLA Ops:
  2.1 23.8 %all-to-all-start.2 = ((s32[32,1,1]{2,1,0:T(1,128)}), s32[32,1,1]{2,1,0:T(1,128)S(1)}, u32[]{:S(2)}, u32[]{:S(2)}) async-start(s32[32,1,1]{2,1,0:T(1,128)} %copy.71), calls=%async_computation.2 | async-start | bytes 32768 | tf_op jit(solution)/shard_map/all_to_all | solution.py:107
  25.9 22.6 %all-to-all-start.1 = ((s32[1,1,128]{1,0,2:T(1,128)}), s32[1,1,128]{1,0,2:T(1,128)S(1)}, u32[]{:S(2)}, u32[]{:S(2)}) async-start(s32[1,1,128]{1,0,2:T(1,128)} %copy.70), calls=%async_computation.1 | async-start | bytes 131072 | tf_op jit(solution)/shard_map/all_to_all | solution.py:180
  48.4 74.7 %all-to-all-start.3 = ((bf16[32,4,1408]{2,1,0:T(4,128)(2,1)}), bf16[32,4,1408]{2,1,0:T(4,128)(2,1)S(1)}, u32[]{:S(2)}, u32[]{:S(2)}) async-start(bf16[32,4,1408]{2,1,0:T(4,128)(2,1)} %reshape.280), calls=%async_computation.3 | async-start | bytes 720896 | tf_op jit(solution)/shard_map/all_to_all | solution.py:106
  123.2 13.5 %copy-start.3 = (bf16[1408,512]{1,0:T(8,128)(2,1)S(1)}, bf16[1408,512]{1,0:T(8,128)(2,1)}, u32[]{:S(2)}) copy-start(bf16[1408,512]{1,0:T(8,128)(2,1)} %param.14) | copy-start | bytes 4325380
  123.2 519.9 %all-to-all-start = ((bf16[2,1408,4096]{1,0,2:T(2,128)(2,1)}), bf16[2,1408,4096]{1,0,2:T(2,128)(2,1)}, u32[]{:S(2)}, u32[]{:S(2)}) async-start(bf16[2,1408,4096]{1,0,2:T(2,128)(2,1)} %copy.68), calls=%async_computation | async-start | bytes 46137344 | tf_op jit(solution)/shard_map/all_to_all | solution.py:179
  130.0 7.5 copy-start.4
  182.2 3.8 copy-start
  186.0 4.0 copy-start.2
  736.1 48.8 %copy-start.1 = (bf16[16,44,512]{2,1,0:T(8,128)(2,1)S(1)}, bf16[16,44,512]{2,1,0:T(8,128)(2,1)}, u32[]{:S(2)}) copy-start(bf16[16,44,512]{2,1,0:T(8,128)(2,1)} %copy-done) | copy-start | bytes 2162692
where the time goes:
time: 1010 us; the launch traced here: 994 us
  waiting for transfers between devices  442 us (44%)
  local copies, waits for them, and re-layouts  240 us (24%)
  matrix products  218 us (22%)
  other arithmetic  67.8 us (7%)
  starting transfers between devices  25.1 us (2%)
    all_to_all x1, waiting for transfers between devices, shards(): lax.all_to_all(outgoing, 'blk', split_axis=2, concat_axis=2, tiled=True)  442 us
    dot_general x2, matrix products, softmax_part(): jnp.einsum('hqk,hdk->hdq', expo, values, precision=lax.Precision.HIGHEST)  129 us
    slice x2, local copies, waits for them, and re-layouts, shards(): cached_keys = blocks_in[0].reshape(heads_here, HD, -1)  93 us
    dot_general x2, matrix products, softmax_part(): jnp.einsum('hdq,hdk->hqk', query_block, keys, preferred_element_type=jnp....  53.4 us
    slice x1, local copies, waits for them, and re-layouts, shards(): cached_values = blocks_in[1].reshape(heads_here, HD, -1).astype(jnp.float32)  48.8 us
    reduce_sum x2, other arithmetic, softmax_part(): total = jnp.sum(expo, axis=2)  45.5 us
    reshape x1, local copies, waits for them, and re-layouts, shards(): outgoing = outgoing.reshape(2, local, table_width * block_len)  42.1 us
    unnamed x12, local copies, waits for them, and re-layouts  20.3 us
  transfers between devices with their start and end apart: 4, of which 1 were waited for; matrix products, arithmetic and copies ran while one was open for 17% of the time, Pallas kernels for 0%

commit v1 on v0

--- a/solution.py
+++ b/solution.py
@@ -1,13 +1,21 @@
+import functools
 import math
 
 import jax
 import jax.numpy as jnp
 from jax import lax
+from jax.experimental import pallas as pl
+from jax.experimental.pallas import tpu as pltpu
 from jax.sharding import PartitionSpec as P
 
 D = 1408
 HD = 88
 BS = 32
+PAIR = 2 * HD
+EXT = PAIR + 16
+LANES = 128
+MASKED = -1e30
+VMEM = 48 * 1024 * 1024
 
 
 masked_score = -1e30
@@ -199,6 +207,458 @@
     return (attended, new_cache)
 
 
+def pack_body(ids, cache_ref, out_ref, *, slots):
+    lane = lax.broadcasted_iota(jnp.int32, (PAIR, LANES), 1) // BS
+
+    def one(w, carry):
+        block = ids[w]
+        start = pl.multiple_of(block // 4 * LANES, LANES)
+        turn = block % 4
+        packed = None
+        for g in range(4):
+            tile = cache_ref[g // 2, g % 2, :, pl.ds(start, LANES)]
+            tile = pltpu.roll(tile, (g + 4 - turn) % 4 * BS, 1)
+            packed = tile if g == 0 else jnp.where(lane == g, tile, packed)
+        out_ref[w] = packed
+        return carry
+
+    lax.fori_loop(0, slots, one, 0, unroll=2)
+
+
+def pack_unit(ids, paged, unit):
+    slots = ids.shape[0]
+    lanes = paged.shape[3]
+    return pl.pallas_call(
+        functools.partial(pack_body, slots=slots),
+        grid_spec=pltpu.PrefetchScalarGridSpec(
+            num_scalar_prefetch=1,
+            grid=(1,),
+            in_specs=[pl.BlockSpec((2, 2, PAIR, lanes), lambda i, s: (0, unit, 0, 0))],
+            out_specs=pl.BlockSpec((slots, PAIR, LANES), lambda i, s: (0, 0, 0)),
+        ),
+        out_shape=jax.ShapeDtypeStruct((slots, PAIR, LANES), jnp.bfloat16),
+        compiler_params=pltpu.CompilerParams(vmem_limit_bytes=VMEM),
+        cost_estimate=pl.CostEstimate(flops=0, bytes_accessed=4500000, transcendentals=0),
+        name="pack_blocks",
+    )(ids, paged)
+
+
+def star_pack_body(ids, *refs):
+    out_ref = refs[8]
+    lane = lax.broadcasted_iota(jnp.int32, (PAIR, LANES), 1) // BS
+    for c in range(2):
+        packed = None
+        for j in range(4):
+            tile = pltpu.roll(refs[c * 4 + j][0, 0], (j + 4 - ids[j] % 4) % 4 * BS, 1)
+            packed = tile if j == 0 else jnp.where(lane == j, tile, packed)
+        out_ref[0, c] = packed
+
+
+def star_pack(ids, paged):
+    pairs = paged.shape[1]
+
+    def spec(c, j):
+        return pl.BlockSpec((1, 1, PAIR, LANES), lambda i, s: (c, pair_of(i), 0, s[j] // 4))
+
+    return pl.pallas_call(
+        star_pack_body,
+        grid_spec=pltpu.PrefetchScalarGridSpec(
+            num_scalar_prefetch=1,
+            grid=(pairs,),
+            in_specs=[spec(c, j) for c in range(2) for j in range(4)],
+            out_specs=pl.BlockSpec((1, 2, PAIR, LANES), lambda i, s: (i, 0, 0, 0)),
+        ),
+        out_shape=jax.ShapeDtypeStruct((pairs, 2, PAIR, LANES), jnp.bfloat16),
+        compiler_params=pltpu.CompilerParams(vmem_limit_bytes=VMEM),
+        name="pack_longest",
+    )(ids, *([paged] * 8))
+
+
+def pair_of(place):
+    return place % 2 * 4 + place // 2 % 2 * 2 + place // 4
+
+
+def project_body(normed_ref, weight_ref, cos_ref, sin_ref, query_ref, cache_ref):
+    normed = normed_ref[...]
+
+    def part(j):
+        return jnp.dot(weight_ref[j], normed, preferred_element_type=jnp.float32)
+
+    def rotate(x):
+        heads = []
+        for h in range(2):
+            one = x[h * HD : (h + 1) * HD]
+            other = jnp.concatenate([one[HD // 2 :], one[: HD // 2]], axis=0)
+            heads.append(one * cos_ref[...] + other * sin_ref[...])
+        return jnp.concatenate(heads, axis=0).astype(jnp.bfloat16)
+
+    query_ref[0] = rotate(part(0))
+    cache_ref[0] = rotate(part(1))
+    cache_ref[1] = part(2).astype(jnp.bfloat16)
+
+
+def project(normed, wqkv, cosine, sine):
+    width, rows = normed.shape
+    pairs = width // PAIR
+    return pl.pallas_call(
+        project_body,
+        grid=(pairs,),
+        in_specs=[
+            pl.BlockSpec((width, rows), lambda i: (0, 0)),
+            pl.BlockSpec((3, PAIR, width), lambda i: (0, i, 0)),
+            pl.BlockSpec((HD, rows), lambda i: (0, 0)),
+            pl.BlockSpec((HD, rows), lambda i: (0, 0)),
+        ],
+        out_specs=[
+            pl.BlockSpec((1, PAIR, rows), lambda i: (i, 0, 0)),
+            pl.BlockSpec((2, PAIR, rows), lambda i: (0, i, 0)),
+        ],
+        out_shape=[
+            jax.ShapeDtypeStruct((pairs, PAIR, rows), jnp.bfloat16),
+            jax.ShapeDtypeStruct((2, width, rows), jnp.bfloat16),
+        ],
+        compiler_params=pltpu.CompilerParams(vmem_limit_bytes=VMEM),
+        cost_estimate=pl.CostEstimate(
+            flops=6 * width * width * rows, bytes_accessed=8 * width * width, transcendentals=0
+        ),
+        name="project_rotate",
+    )(normed, wqkv, cosine, sine)
+
+
+def split_three(x):
+    high = x.astype(jnp.bfloat16).astype(jnp.float32)
+    middle = (x - high).astype(jnp.bfloat16).astype(jnp.float32)
+    return high, middle, x - high - middle
+
+
+def attend_pair(query, keys, values, old, own, out):
+    rows = query.shape[1]
+    step = min(256, rows)
+    extra = jnp.where(lax.broadcasted_iota(jnp.int32, (EXT - PAIR, rows), 0) == 0, 1.0, 0.0)
+    turned = jnp.transpose(jnp.concatenate([query, extra.astype(jnp.bfloat16)], axis=0))
+    column = lax.broadcasted_iota(jnp.int32, (step, EXT), 1)
+    ahead = lax.broadcasted_iota(jnp.int32, (step, step), 1) > lax.broadcasted_iota(jnp.int32, (step, step), 0)
+    factor = math.log2(math.e) * HD ** (-0.5)
+    for first in range(0, rows, step):
+        count = old + (first + step if own else 0)
+        parts = []
+        for h in range(2):
+            used = (column // HD == h) | (column == PAIR)
+            mine = jnp.where(used, turned[first : first + step], 0).astype(jnp.bfloat16)
+            scores = jnp.dot(mine, keys[:, :count], preferred_element_type=jnp.float32)
+            if own:
+                last = jnp.where(ahead, MASKED, scores[:, count - step :])
+                scores = jnp.concatenate([scores[:, : count - step], last], axis=1)
+            highest = jnp.max(scores, axis=1, keepdims=True)
+            expo = jnp.exp2((scores - highest) * factor).astype(jnp.bfloat16)
+            mixed = lax.dot_general(
+                expo, values[:, :count], (((1,), (1,)), ((), ())), preferred_element_type=jnp.float32
+            )
+            total = mixed[:, PAIR : PAIR + 1]
+            parts.append((mixed / total, split_three(highest * factor + jnp.log2(total))))
+        result = jnp.where(column < HD, parts[0][0], parts[1][0])
+        for h in range(2):
+            for j in range(3):
+                result = jnp.where(column == PAIR + 2 * j + h, parts[h][1][j], result)
+        result = jnp.where(column >= PAIR + 6, 0.0, result)
+        out[:, first : first + step] = jnp.transpose(result).astype(jnp.bfloat16)
+
+
+def attend_body(arrived_ref, bias_ref, query_ref, own_ref, out_ref, kv, *, own_rows):
+    old = bias_ref.shape[1]
+    lower = lax.broadcasted_iota(jnp.int32, (EXT - PAIR, old + own_rows), 0)
+    masks = jnp.concatenate([bias_ref[...], jnp.zeros((1, own_rows), jnp.float32)], axis=1)
+    for g in range(2):
+        kv[g, PAIR:EXT] = jnp.where(lower == 0, masks, 0.0).astype(jnp.bfloat16)
+        kv[2 + g, PAIR:EXT] = jnp.where(lower == 0, 1.0, 0.0).astype(jnp.bfloat16)
+        kv[g, 0:PAIR, old:] = own_ref[0, g * PAIR : (g + 1) * PAIR]
+        kv[2 + g, 0:PAIR, old:] = own_ref[1, g * PAIR : (g + 1) * PAIR]
+    for t in range(old // LANES):
+        tiles = [arrived_ref[4 * t + j] for j in range(4)]
+        for g in range(4):
+            kv[g, 0:PAIR, t * LANES : (t + 1) * LANES] = jnp.concatenate(
+                [tile[:, g * BS : (g + 1) * BS] for tile in tiles], axis=1
+            )
+    for g in range(2):
+        attend_pair(query_ref[g], kv.at[g], kv.at[2 + g], old, True, out_ref.at[g])
+
+
+def attend_unit(arrived, bias, queries, new_cache, unit):
+    rows = queries.shape[2]
+    old = bias.shape[1]
+    work = 4 * rows * (old + rows)
+    return pl.pallas_call(
+        functools.partial(attend_body, own_rows=rows),
+        grid=(1,),
+        in_specs=[
+            pl.BlockSpec(arrived.shape, lambda i: (0, 0, 0)),
+            pl.BlockSpec((1, old), lambda i: (0, 0)),
+            pl.BlockSpec((2, PAIR, rows), lambda i: (unit, 0, 0)),
+            pl.BlockSpec((2, 2 * PAIR, rows), lambda i: (0, unit, 0)),
+        ],
+        out_specs=pl.BlockSpec((2, EXT, rows), lambda i: (0, 0, 0)),
+        out_shape=jax.ShapeDtypeStruct((2, EXT, rows), jnp.bfloat16),
+        scratch_shapes=[pltpu.VMEM((4, EXT, old + rows), jnp.bfloat16)],
+        compiler_params=pltpu.CompilerParams(vmem_limit_bytes=VMEM),
+        cost_estimate=pl.CostEstimate(
+            flops=work * 1024, bytes_accessed=4000000, transcendentals=work
+        ),
+        name="attend_heads",
+    )(arrived, bias, queries, new_cache)
+
+
+def star_body(arrived_ref, query_ref, out_ref, kv, *, sources):
+    lower = lax.broadcasted_iota(jnp.int32, (EXT - PAIR, sources * LANES), 0)
+    kv[0, PAIR:EXT] = jnp.zeros(lower.shape, jnp.bfloat16)
+    kv[1, PAIR:EXT] = jnp.where(lower == 0, 1.0, 0.0).astype(jnp.bfloat16)
+    for s in range(sources):
+        for c in range(2):
+            kv[c, 0:PAIR, s * LANES : (s + 1) * LANES] = arrived_ref[s, c]
+    attend_pair(query_ref[...], kv.at[0], kv.at[1], sources * LANES, False, out_ref)
+
+
+def star_attend(arrived, query):
+    sources = arrived.shape[0]
+    rows = query.shape[1]
+    work = 2 * rows * sources * LANES
+    return pl.pallas_call(
+        functools.partial(star_body, sources=sources),
+        out_shape=jax.ShapeDtypeStruct((EXT, rows), jnp.bfloat16),
+        scratch_shapes=[pltpu.VMEM((2, EXT, sources * LANES), jnp.bfloat16)],
+        compiler_params=pltpu.CompilerParams(vmem_limit_bytes=VMEM),
+        cost_estimate=pl.CostEstimate(
+            flops=work * 1024, bytes_accessed=1500000, transcendentals=work
+        ),
+        name="attend_longest",
+    )(arrived, query)
+
+
+def fold_two(first, second):
+    def logs(x):
+        return [x[PAIR + h : PAIR + h + 1] + x[PAIR + 2 + h : PAIR + 3 + h] + x[PAIR + 4 + h : PAIR + 5 + h] for h in range(2)]
+
+    logs_a, logs_b = logs(first), logs(second)
+    heads, below = [], []
+    for h in range(2):
+        top = jnp.maximum(logs_a[h], logs_b[h])
+        share_a, share_b = jnp.exp2(logs_a[h] - top), jnp.exp2(logs_b[h] - top)
+        total = share_a + share_b
+        span = slice(h * HD, (h + 1) * HD)
+        heads.append((first[span] * share_a + second[span] * share_b) / total)
+        below.append(split_three(top + jnp.log2(total)))
+    return heads, below
+
+
+def fold_body(first_ref, second_ref, out_ref):
+    heads, below = fold_two(first_ref[...].astype(jnp.float32), second_ref[...].astype(jnp.float32))
+    row = lax.broadcasted_iota(jnp.int32, (EXT - PAIR, out_ref.shape[1]), 0)
+    lower = jnp.zeros(row.shape, jnp.float32)
+    for j in range(3):
+        for h in range(2):
+            lower = jnp.where(row == 2 * j + h, below[h][j], lower)
+    out_ref[...] = jnp.concatenate(heads + [lower], axis=0).astype(jnp.bfloat16)
+
+
+def fold(first, second):
+    return pl.pallas_call(
+        fold_body,
+        out_shape=jax.ShapeDtypeStruct(first.shape, jnp.bfloat16),
+        compiler_params=pltpu.CompilerParams(vmem_limit_bytes=VMEM),
+        name="fold_parts",
+    )(first, second)
+
+
+def finish_body(flag, star_ref, *refs):
+    out_ref = refs[-1]
+    for u, unit_ref in enumerate(refs[:-1]):
+        for g in range(2):
+            pair = 2 * u + g
+            span = pl.ds(pair * PAIR, PAIR)
+            out_ref[span] = unit_ref[g, 0:PAIR]
+
+            @pl.when(flag[0] == 1)
+            def _():
+                heads, _ = fold_two(unit_ref[g].astype(jnp.float32), star_ref[pair].astype(jnp.float32))
+                out_ref[span] = jnp.concatenate(heads, axis=0).astype(jnp.bfloat16)
+
+
+def finish(flag, star, units):
+    pairs, _, rows = star.shape
+    whole = [pl.BlockSpec(star.shape, lambda i, s: (0, 0, 0))]
+    return pl.pallas_call(
+        finish_body,
+        grid_spec=pltpu.PrefetchScalarGridSpec(
+            num_scalar_prefetch=1,
+            grid=(1,),
+            in_specs=whole + [pl.BlockSpec(u.shape, lambda i, s: (0, 0, 0)) for u in units],
+            out_specs=pl.BlockSpec((pairs * PAIR, rows), lambda i, s: (0, 0)),
+        ),
+        out_shape=jax.ShapeDtypeStruct((pairs * PAIR, rows), jnp.bfloat16),
+        compiler_params=pltpu.CompilerParams(vmem_limit_bytes=VMEM),
+        name="finish_heads",
+    )(flag, star, *units)
+
+
+def place_and_norm(vision, ln_gain, merge_proj, image_slot, text, rms_gain):
+    groups = vision.shape[2]
+    width = vision.shape[1]
+    floats = vision.astype(jnp.float32)
+    average = jnp.sum(floats, axis=1) / D
+    spread = jnp.sum(floats * floats, axis=1) / D - average * average
+    normed_vision = (
+        (floats - average[:, None, :])
+        * lax.rsqrt(spread + 1e-06)[:, None, :]
+        * ln_gain[None, :, None]
+    ).astype(jnp.bfloat16)
+    merged = jnp.einsum(
+        "tcd,tcg->gd", merge_proj, normed_vision, preferred_element_type=jnp.float32
+    ).astype(jnp.bfloat16)
+    devices = lax.axis_size("blk")
+    rows_here = text.shape[1]
+    pieces = image_slot.shape[0]
+    piece_rows = groups // pieces
+    lines = jnp.arange(rows_here, dtype=jnp.int32)
+    offsets = jnp.arange(piece_rows, dtype=jnp.int32)
+    target = image_slot // rows_here
+    within = image_slot % rows_here
+    select = target[None, :] == jnp.arange(devices, dtype=jnp.int32)[:, None]
+    outbound = (
+        jnp.dot(
+            select.astype(jnp.bfloat16),
+            merged.reshape(pieces, piece_rows * width),
+            preferred_element_type=jnp.float32,
+        )
+        .astype(jnp.bfloat16)
+        .reshape(devices, piece_rows, width)
+    )
+    starts = jnp.sum(jnp.where(select, within[None, :] + 1, 0), axis=1) - 1
+    arrived = lax.all_to_all(outbound, "blk", split_axis=0, concat_axis=0, tiled=True)
+    arrived_start = lax.all_to_all(starts, "blk", split_axis=0, concat_axis=0, tiled=True)
+    row_ids = (arrived_start[:, None] + offsets[None, :]).reshape(-1)
+    present = jnp.repeat(arrived_start >= 0, piece_rows)
+    hits = (row_ids[:, None] == lines[None, :]) & present[:, None]
+    placed_rows = jnp.einsum(
+        "kl,kr->lr",
+        arrived.reshape(devices * piece_rows, width),
+        hits.astype(jnp.bfloat16),
+        preferred_element_type=jnp.float32,
+    ).astype(jnp.bfloat16)
+    covered = jnp.any(hits, axis=0)
+    placed = jnp.where(covered[None, :], placed_rows, text)
+    row_floats = placed.astype(jnp.float32)
+    square_sums = jnp.sum(row_floats * row_floats, axis=0)
+    return (row_floats * lax.rsqrt(square_sums / D + 1e-06)[None, :] * rms_gain[:, None]).astype(
+        jnp.bfloat16
+    )
+
+
+def rotary_tables(places):
+    half = HD // 2
+    freq_index = jnp.arange(half, dtype=jnp.float32)
+    inverse = jnp.exp(freq_index * (-2.0 * math.log(10000.0) / HD))
+    angles = inverse[:, None] * places[None, :]
+    cosine = jnp.cos(angles)
+    sine = jnp.sin(angles)
+    return jnp.concatenate([cosine, cosine], axis=0), jnp.concatenate([-sine, sine], axis=0)
+
+
+def swap(x, bit):
+    size = lax.axis_size("blk")
+    return lax.ppermute(x, "blk", [(i, i ^ (1 << bit)) for i in range(size)])
+
+
+def spread_shards(
+    vision, ln_gain, merge_proj, image_slot, text, rms_gain, wqkv, pcache, block_table, cache_len
+):
+    devices = lax.axis_size("blk")
+    here = lax.axis_index("blk")
+    width, rows = text.shape
+    pairs = width // PAIR
+    owned = pcache.shape[2] // BS
+    table_width = block_table.shape[1]
+    each = table_width // devices
+
+    holder = jnp.where(block_table >= 0, block_table // owned, -1)
+    local = block_table - here * owned
+    mine = holder == here
+    longest = jnp.argmax(block_table[:, table_width - 1]).astype(jnp.int32)
+    chosen = jnp.max(jnp.where(mine, local, 0), axis=1)
+    star_row = jnp.where(
+        lax.dynamic_index_in_dim(mine, longest, 0, False),
+        lax.dynamic_index_in_dim(local, longest, 0, False),
+        -1,
+    )
+    rank = jnp.sum((star_row[None, :] > star_row[:, None]).astype(jnp.int32), axis=1)
+    star_ids = jnp.sum(
+        jnp.where(
+            (rank[None, :] == jnp.arange(each, dtype=jnp.int32)[:, None]) & (star_row >= 0)[None, :],
+            star_row[None, :],
+            0,
+        ),
+        axis=1,
+    )
+    row_holder = lax.dynamic_index_in_dim(holder, here, 0, False)
+    row_count = jnp.clip(cache_len[0] - BS * jnp.arange(table_width, dtype=jnp.int32), 0, BS)
+    live = jnp.sum(
+        jnp.where(
+            row_holder[None, :] == jnp.arange(devices, dtype=jnp.int32)[:, None], row_count[None, :], 0
+        ),
+        axis=1,
+    )
+    live = jnp.where(here == longest, 0, live)
+    bias = jnp.where(jnp.arange(BS, dtype=jnp.int32)[None, :] < live[:, None], 0.0, MASKED)
+    bias = bias.astype(jnp.float32).reshape(1, devices * BS)
+
+    paged = pcache.reshape(2, pairs, PAIR, owned * BS)
+    units = pairs // 2
+    planes = [[p * pairs + i for i in range(pairs)] for p in range(devices // pairs)]
+
+    def exchange(x, groups=None):
+        return lax.all_to_all(x, "blk", split_axis=0, concat_axis=0, tiled=True, axis_index_groups=groups)
+
+    arrived = []
+    for u in range(units):
+        arrived.append(exchange(pack_unit(chosen, paged, u)))
+    star_kv = exchange(star_pack(star_ids, paged), planes)
+
+    normed = place_and_norm(vision, ln_gain, merge_proj, image_slot, text, rms_gain)
+    places = (cache_len[0] + jnp.arange(rows, dtype=jnp.int32)).astype(jnp.float32)
+    queries, new_cache = project(normed, wqkv, *rotary_tables(places))
+
+    query = queries
+    plane_bits = pairs.bit_length() - 1
+    all_bits = devices.bit_length() - 1
+    for bit in range(plane_bits):
+        mine_bit, star_bit = (here >> bit) & 1, (longest >> bit) & 1
+        halves = query.reshape(2, query.shape[0] // 2, PAIR, rows)
+        kept = lax.dynamic_index_in_dim(halves, mine_bit, 0, False)
+        given = lax.dynamic_index_in_dim(halves, 1 - mine_bit, 0, False)
+        query = jnp.where(star_bit == mine_bit, kept, swap(given, bit))
+    for bit in range(plane_bits, all_bits):
+        same = ((here ^ longest) >> bit) & 1
+        query = jnp.where(same == 0, query, swap(query, bit))
+    star = star_attend(star_kv, query[0])
+    for bit in range(plane_bits, all_bits):
+        star = fold(star, swap(star, bit))
+    star = star[None]
+    for bit in reversed(range(plane_bits)):
+        other = swap(star, bit)
+        mine_bit = (here >> bit) & 1
+        star = jnp.where(
+            mine_bit == 0, jnp.concatenate([star, other]), jnp.concatenate([other, star])
+        )
+
+    results = [attend_unit(arrived[u], bias, queries, new_cache, u) for u in range(units)]
+    flag = (here == longest).astype(jnp.int32).reshape(1)
+    return (finish(flag, star, results), new_cache)
+
+
+def spreads(mesh):
+    devices = mesh.shape["blk"]
+    pairs = D // PAIR
+    return mesh.shape["head"] == 1 and devices % pairs == 0 and devices & (devices - 1) == 0
+
+
 def solution(mesh):
     in_specs = (
         P(None, "head", "blk"),
@@ -213,4 +673,5 @@
         P("blk"),
     )
     out_specs = (P("head", "blk"), P(None, "head", "blk"))
-    return jax.shard_map(shards, mesh=mesh, in_specs=in_specs, out_specs=out_specs, check_vma=False)
+    body = spread_shards if spreads(mesh) else shards
+    return jax.shard_map(body, mesh=mesh, in_specs=in_specs, out_specs=out_specs, check_vma=False)

time: 1010 us -> 301 us (0.30); the launches traced: 994 us -> 299 us
  waiting for transfers between devices: 442 us -> 136 us
  local copies, waits for them, and re-layouts: 240 us -> 17.2 us
  matrix products: 218 us -> 10.9 us
  Pallas kernels: 0 us -> 72 us
  other arithmetic: 67.8 us -> 16.5 us
  starting transfers between devices: 25.1 us -> 39.8 us
    all_to_all x4 -> x7, waiting for transfers between devices: 442 us -> 58.5 us  [the longest x5 52.1 us: exchange(): lax.all_to_all(x, 'blk', split_axis=0, concat_axis=0, tiled=True, axis_in...]
    dot_general x9 -> x3, matrix products: 218 us -> 10.9 us  [the longest x1 8.35 us: place_and_norm(): jnp.einsum('tcd,tcg->gd', merge_proj, normed_vision, preferred_element_ty...]
    slice x7 -> x1, local copies, waits for them, and re-layouts: 156 us -> 0.9 us  [spread_shards(): longest = jnp.argmax(block_table[:, table_width - 1]).astype(jnp.int32)]
    ppermute x0 -> x10, waiting for transfers between devices: none -> 77.6 us  [swap(): return lax.ppermute(x, 'blk', [(i, i ^ 1 << bit) for i in range(size)])]
    pallas_call x0 -> x14, Pallas kernels: none -> 72 us  [the longest x4 24.8 us: attend_unit(): pl.pallas_call(functools.partial(attend_body, own_rows=rows), grid=(1,),...]
    reduce_sum x8 -> x5, other arithmetic: 49.4 us -> 1.87 us  [the longest x1 1.38 us: place_and_norm(): average = jnp.sum(floats, axis=1) / D]
    reshape x4 -> x3, local copies, waits for them, and re-layouts: 43.2 us -> 2.77 us  [the longest x1 1.81 us: place_and_norm(): arrived.reshape(devices * piece_rows, width)]
    convert_element_type x3 -> x0, local copies, waits for them, and re-layouts: 18.6 us -> none  [the longest x1 15.5 us: shards(): outgoing = jnp.einsum('wo,cfob->cfwb', routing.astype(jnp.bfloat16), page...]
  transfers between devices with their start and end apart: 4 -> 17, of which waited for: 1 -> 12; matrix products, arithmetic and copies ran while one was open for 17% -> 10% of each run, Pallas kernels for 0% -> 24%
where the time goes in v1:
time: 301 us; the launch traced here: 299 us
  waiting for transfers between devices  136 us (45%)
  Pallas kernels  72 us (24%)
  starting transfers between devices  39.8 us (13%)
  local copies, waits for them, and re-layouts  17.2 us (6%)
  other arithmetic  16.5 us (5%)
  matrix products  10.9 us (4%)
  between operations  6.81 us (2%)
    ppermute x10, waiting for transfers between devices, swap(): return lax.ppermute(x, 'blk', [(i, i ^ 1 << bit) for i in range(size)])  77.6 us
    all_to_all x5, waiting for transfers between devices, exchange(): lax.all_to_all(x, 'blk', split_axis=0, concat_axis=0, tiled=True, axis_in...  52.1 us
    pallas_call x4, Pallas kernels, attend_unit(): pl.pallas_call(functools.partial(attend_body, own_rows=rows), grid=(1,),...  24.8 us
    pallas_call x4, Pallas kernels, pack_unit(): pl.pallas_call(functools.partial(pack_body, slots=slots), grid_spec=pltpu...  24.7 us
    all_to_all x5, starting transfers between devices, exchange(): lax.all_to_all(x, 'blk', split_axis=0, concat_axis=0, tiled=True, axis_in...  17.5 us
    pallas_call x1, Pallas kernels, project(): pl.pallas_call(project_body, grid=(pairs,), in_specs=[pl.BlockSpec((width...  12.2 us
    ppermute x10, starting transfers between devices, swap(): return lax.ppermute(x, 'blk', [(i, i ^ 1 << bit) for i in range(size)])  11 us
    unnamed x36, local copies, waits for them, and re-layouts  10.5 us
  transfers between devices with their start and end apart: 17, of which 12 were waited for; matrix products, arithmetic and copies ran while one was open for 10% of the time, Pallas kernels for 24%

profile of v1, /device:TPU:0, one launch (start us, length us, event | category | flops | bytes accessed | tf_op | source)
XLA Modules:
  0.0 299.2 jit_solution(4849995884633856266)
XLA Ops:
  2.1 7.3 %all-to-all-start.1 = ((s32[32,1,1]{2,1,0:T(1,128)}), s32[32,1,1]{2,1,0:T(1,128)S(1)}, u32[]{:S(2)}, u32[]{:S(2)}) async-start(s32[32,1,1]{2,1,0:T(1,128)} %copy.14), calls=%async_computation.1 | async-start | bytes 32768 | tf_op jit(solution)/shard_map/all_to_all | solution.py:536
  9.4 1.4 convert_reduce_fusion
  15.4 6.6 %pack_longest.1 = bf16[8,2,176,128]{3,2,1,0:T(8,128)(2,1)} custom-call(s32[4]{0:T(128)S(1)} %select_reduce_fusion.3.ids, bf16[2,8,176,2048]{3,2,1,0:T(8,128)(2,1)} %bitcast.36, bf16[2,8,176,2048]{3,2,1,0:T(8,128)(2,1)} %bitcast.37, bf16[2,8,176,2048]{3,2,1,0:T(8,128)(2,1)} %bitcast.38, bf16[2,8,176,2048]{3,2,1,0:T(8,128)(2,1)} %bitcast.39, ...), custom_call_target="tpu_custom_call" | custom-call | tf_op jit(solution)/shard_map/pack_longest/pallas_call | solution.py:263
  22.1 4.1 %all-to-all-start = ((bf16[8,2,176,128]{3,2,1,0:T(8,128)(2,1)}), bf16[8,2,176,128]{3,2,1,0:T(8,128)(2,1)S(1)}, u32[]{:S(2)}, u32[]{:S(2)}) async-start(bf16[8,2,176,128]{3,2,1,0:T(8,128)(2,1)} %pack_longest.1), calls=%async_computation | async-start | bytes 1441792 | tf_op jit(solution)/shard_map/all_to_all | solution.py:617
  26.2 8.4 %fusion.4 = bf16[64,1408]{1,0:T(8,128)(2,1)S(1)} fusion(bf16[4,1408,1408]{2,1,0:T(8,128)(2,1)} %param.12, bf16[4,1408,64]{1,2,0:T(8,128)(2,1)S(1)} %copy-done.14, f32[1408]{0:T(1024)S(1)} %copy-done.16, f32[4,64]{1,0:T(4,128)S(1)} %get-tuple-element.20, f32[4,64]{1,0:T(4,128)S(1)} %get-tuple-element.19), kind=kOutput, calls=%fused_computation.9 | convolution fusion | flops 1016913920 | bytes 16768512 | tf_op jit(solution)/shard_map/tcd,tcg->gd/dot_general | solution.py:513
  35.9 2.2 all-to-all-done.arrived_ref
  38.9 4.0 %all-to-all-start.2 = ((bf16[32,4,1408]{2,1,0:T(4,128)(2,1)}), bf16[32,4,1408]{2,1,0:T(4,128)(2,1)S(1)}, u32[]{:S(2)}, u32[]{:S(2)}) async-start(bf16[32,4,1408]{2,1,0:T(4,128)(2,1)} %reshape.147), calls=%async_computation.2 | async-start | bytes 720896 | tf_op jit(solution)/shard_map/all_to_all | solution.py:535
  43.0 6.2 %pack_blocks.5 = bf16[32,176,128]{2,1,0:T(8,128)(2,1)} custom-call(s32[32]{0:T(128)S(1)} %get-tuple-element.10.ids, bf16[2,8,176,2048]{3,2,1,0:T(8,128)(2,1)} %bitcast.44), custom_call_target="tpu_custom_call" | custom-call | bytes 4500000 | tf_op jit(solution)/shard_map/pack_blocks/pallas_call | solution.py:231
  49.1 6.4 %all-to-all-done.2 = bf16[32,4,1408]{2,1,0:T(4,128)(2,1)S(1)} async-done(((bf16[32,4,1408]{2,1,0:T(4,128)(2,1)}), bf16[32,4,1408]{2,1,0:T(4,128)(2,1)S(1)}, u32[]{:S(2)}, u32[]{:S(2)}) %all-to-all-start.2) | async-done | bytes 360480 | tf_op jit(solution)/shard_map/all_to_all | solution.py:535
  55.5 2.7 all-to-all-start.4
  58.2 6.2 %pack_blocks.6 = bf16[32,176,128]{2,1,0:T(8,128)(2,1)} custom-call(s32[32]{0:T(128)S(1)} %get-tuple-element.10.ids, bf16[2,8,176,2048]{3,2,1,0:T(8,128)(2,1)} %bitcast.45), custom_call_target="tpu_custom_call" | custom-call | bytes 4500000 | tf_op jit(solution)/shard_map/pack_blocks/pallas_call | solution.py:231
  64.4 28.9 %all-to-all-done.4.arrived_ref = bf16[32,176,128]{2,1,0:T(8,128)(2,1)S(1)} async-done(((bf16[32,176,128]{2,1,0:T(8,128)(2,1)}), bf16[32,176,128]{2,1,0:T(8,128)(2,1)S(1)}, u32[]{:S(2)}, u32[]{:S(2)}) %all-to-all-start.4) | async-done | bytes 1441824 | tf_op jit(solution)/shard_map/all_to_all | solution.py:617
  93.3 3.4 %all-to-all-start.5 = ((bf16[32,176,128]{2,1,0:T(8,128)(2,1)}), bf16[32,176,128]{2,1,0:T(8,128)(2,1)S(1)}, u32[]{:S(2)}, u32[]{:S(2)}) async-start(bf16[32,176,128]{2,1,0:T(8,128)(2,1)} %pack_blocks.6), calls=%async_computation.5 | async-start | bytes 2883584 | tf_op jit(solution)/shard_map/all_to_all | solution.py:617
  96.7 6.2 %pack_blocks.7 = bf16[32,176,128]{2,1,0:T(8,128)(2,1)} custom-call(s32[32]{0:T(128)S(1)} %get-tuple-element.10.ids, bf16[2,8,176,2048]{3,2,1,0:T(8,128)(2,1)} %bitcast.46), custom_call_target="tpu_custom_call" | custom-call | bytes 4500000 | tf_op jit(solution)/shard_map/pack_blocks/pallas_call | solution.py:231
  105.3 1.8 reshape.148
  107.1 2.2 fusion
  109.3 1.5 fusion.2.normed_ref
  110.8 21.0 %all-to-all-done.5.arrived_ref = bf16[32,176,128]{2,1,0:T(8,128)(2,1)S(1)} async-done(((bf16[32,176,128]{2,1,0:T(8,128)(2,1)}), bf16[32,176,128]{2,1,0:T(8,128)(2,1)S(1)}, u32[]{:S(2)}, u32[]{:S(2)}) %all-to-all-start.5) | async-done | bytes 1441824 | tf_op jit(solution)/shard_map/all_to_all | solution.py:617
  131.8 3.7 %all-to-all-start.6 = ((bf16[32,176,128]{2,1,0:T(8,128)(2,1)}), bf16[32,176,128]{2,1,0:T(8,128)(2,1)}, u32[]{:S(2)}, u32[]{:S(2)}) async-start(bf16[32,176,128]{2,1,0:T(8,128)(2,1)} %pack_blocks.7), calls=%async_computation.6 | async-start | bytes 2883584 | tf_op jit(solution)/shard_map/all_to_all | solution.py:617
  135.5 1.4 copy-done
  136.9 12.2 %project_rotate.1 = (bf16[8,176,512]{2,1,0:T(8,128)(2,1)S(1)}, bf16[2,1408,512]{2,1,0:T(8,128)(2,1)}) custom-call(bf16[1408,512]{1,0:T(8,128)(2,1)S(1)} %copy-done, bf16[3,1408,1408]{2,1,0:T(8,128)(2,1)} %weight_ref.1, f32[88,512]{1,0:T(8,128)S(1)} %get-tuple-element.25.cos_ref, f32[88,512]{1,0:T(8,128)S(1)} %get-tuple-element.26.sin_ref), custom_call_target="tpu_custom_call" | custom-call | flops 6090129408 | bytes 15859712 | tf_op jit(solution)/shard_map/project_rotate/pallas_call | solution.py:303
  151.9 1.7 collective-permute-done
  153.6 2.0 bitcast_select_fusion
  156.7 1.8 collective-permute-start.1
  159.1 10.4 %collective-permute-done.1 = bf16[2,176,512]{2,1,0:T(8,128)(2,1)} collective-permute-done((bf16[2,176,512]{2,1,0:T(8,128)(2,1)S(1)}, bf16[2,176,512]{2,1,0:T(8,128)(2,1)}, u32[]{:S(2)}, u32[]{:S(2)}) %collective-permute-start.1) | collective-permute-done | bytes 360480 | tf_op jit(solution)/shard_map/ppermute | solution.py:567
  169.5 1.1 bitcast_select_fusion.1
  170.7 2.2 collective-permute-start.2
  173.5 3.7 %collective-permute-done.2 = bf16[1,176,512]{2,1,0:T(8,128)(2,1)} collective-permute-done((bf16[1,176,512]{2,1,0:T(8,128)(2,1)S(1)}, bf16[1,176,512]{2,1,0:T(8,128)(2,1)}, u32[]{:S(2)}, u32[]{:S(2)}) %collective-permute-start.2) | collective-permute-done | bytes 180256 | tf_op jit(solution)/shard_map/ppermute | solution.py:567
  178.2 1.8 collective-permute-start.3
  179.9 6.2 %pack_blocks.4 = bf16[32,176,128]{2,1,0:T(8,128)(2,1)} custom-call(s32[32]{0:T(128)S(1)} %get-tuple-element.10.ids, bf16[2,8,176,2048]{3,2,1,0:T(8,128)(2,1)} %bitcast.47), custom_call_target="tpu_custom_call" | custom-call | bytes 4500000 | tf_op jit(solution)/shard_map/pack_blocks/pallas_call | solution.py:231
  186.1 3.6 %all-to-all-start.3 = ((bf16[32,176,128]{2,1,0:T(8,128)(2,1)}), bf16[32,176,128]{2,1,0:T(8,128)(2,1)}, u32[]{:S(2)}, u32[]{:S(2)}) async-start(bf16[32,176,128]{2,1,0:T(8,128)(2,1)} %pack_blocks.4), calls=%async_computation.3 | async-start | bytes 2883584 | tf_op jit(solution)/shard_map/all_to_all | solution.py:617
  190.4 2.7 collective-permute-start.4
  193.0 39.2 %collective-permute-done.4 = bf16[1,176,512]{2,1,0:T(8,128)(2,1)S(1)} collective-permute-done((bf16[1,176,512]{2,1,0:T(8,128)(2,1)S(1)}, bf16[1,176,512]{2,1,0:T(8,128)(2,1)S(1)}, u32[]{:S(2)}, u32[]{:S(2)}) %collective-permute-start.4) | collective-permute-done | bytes 180256 | tf_op jit(solution)/shard_map/ppermute | solution.py:567
  233.3 2.3 attend_longest.1.first_ref
  236.3 5.8 %collective-permute-done.5.second_ref = bf16[192,512]{1,0:T(8,128)(2,1)S(1)} collective-permute-done((bf16[192,512]{1,0:T(8,128)(2,1)S(1)}, bf16[192,512]{1,0:T(8,128)(2,1)S(1)}, u32[]{:S(2)}, u32[]{:S(2)}) %collective-permute-start.5) | collective-permute-done | bytes 196640 | tf_op jit(solution)/shard_map/ppermute | solution.py:567
  242.6 10.4 %collective-permute-done.6.second_ref = bf16[192,512]{1,0:T(8,128)(2,1)S(1)} collective-permute-done((bf16[192,512]{1,0:T(8,128)(2,1)S(1)}, bf16[192,512]{1,0:T(8,128)(2,1)S(1)}, u32[]{:S(2)}, u32[]{:S(2)}) %collective-permute-start.6) | collective-permute-done | bytes 196640 | tf_op jit(solution)/shard_map/ppermute | solution.py:567
  253.1 1.1 collective-permute-start.7
  254.2 5.7 %collective-permute-done.7 = bf16[1,192,512]{2,1,0:T(8,128)(2,1)S(1)} collective-permute-done((bf16[1,192,512]{2,1,0:T(8,128)(2,1)S(1)}, bf16[1,192,512]{2,1,0:T(8,128)(2,1)S(1)}, u32[]{:S(2)}, u32[]{:S(2)}) %collective-permute-start.7) | collective-permute-done | bytes 196640 | tf_op jit(solution)/shard_map/ppermute | solution.py:567
  261.9 1.4 copy-done.2
  263.3 1.8 copy-done.11
  265.1 5.4 %attend_heads.5.refs_1_ = bf16[2,192,512]{2,1,0:T(8,128)(2,1)S(1)} custom-call(bf16[32,176,128]{2,1,0:T(8,128)(2,1)S(1)} %all-to-all-done.4.arrived_ref, f32[1,1024]{1,0:T(1,128)S(1)} %select_n.208.bias_ref, bf16[8,176,512]{2,1,0:T(8,128)(2,1)S(1)} %copy-done.2, bf16[2,1408,512]{2,1,0:T(8,128)(2,1)S(1)} %copy-done.11), custom_call_target="tpu_custom_call" | custom-call | flops 3221225472 | bytes 4000000 | tf_op jit(solution)/shard_map/attend_heads/pallas_call | solution.py:390
  271.2 2.4 maximum_select_fusion.1
  273.5 5.7 %attend_heads.6.refs_2_ = bf16[2,192,512]{2,1,0:T(8,128)(2,1)S(1)} custom-call(bf16[32,176,128]{2,1,0:T(8,128)(2,1)S(1)} %all-to-all-done.5.arrived_ref, f32[1,1024]{1,0:T(1,128)S(1)} %select_n.208.bias_ref, bf16[8,176,512]{2,1,0:T(8,128)(2,1)S(1)} %copy-done.3, bf16[2,1408,512]{2,1,0:T(8,128)(2,1)S(1)} %copy-done.11), custom_call_target="tpu_custom_call" | custom-call | flops 3221225472 | bytes 4000000 | tf_op jit(solution)/shard_map/attend_heads/pallas_call | solution.py:390
  280.0 6.9 %attend_heads.7.refs_3_ = bf16[2,192,512]{2,1,0:T(8,128)(2,1)S(1)} custom-call(bf16[32,176,128]{2,1,0:T(8,128)(2,1)} %all-to-all-done.6.arrived_ref, f32[1,1024]{1,0:T(1,128)S(1)} %select_n.208.bias_ref, bf16[8,176,512]{2,1,0:T(8,128)(2,1)S(1)} %copy-done.3, bf16[2,1408,512]{2,1,0:T(8,128)(2,1)S(1)} %copy-done.12), custom_call_target="tpu_custom_call" | custom-call | flops 3221225472 | bytes 4000000 | tf_op jit(solution)/shard_map/attend_heads/pallas_call | solution.py:390
  287.7 1.4 copy-done.4
  289.0 6.8 %attend_heads.4.refs_0_ = bf16[2,192,512]{2,1,0:T(8,128)(2,1)S(1)} custom-call(bf16[32,176,128]{2,1,0:T(8,128)(2,1)} %all-to-all-done.3.arrived_ref, f32[1,1024]{1,0:T(1,128)S(1)} %select_n.208.bias_ref, bf16[8,176,512]{2,1,0:T(8,128)(2,1)S(1)} %copy-done.4, bf16[2,1408,512]{2,1,0:T(8,128)(2,1)S(1)} %copy-done.13), custom_call_target="tpu_custom_call" | custom-call | flops 3221225472 | bytes 4000000 | tf_op jit(solution)/shard_map/attend_heads/pallas_call | solution.py:390
  295.9 2.2 maximum_select_fusion.star_ref
  298.0 1.2 finish_heads.1
  (84 shorter events, 18.2 us)
Async XLA Ops:
  2.1 20.0 %all-to-all-start.1 = ((s32[32,1,1]{2,1,0:T(1,128)}), s32[32,1,1]{2,1,0:T(1,128)S(1)}, u32[]{:S(2)}, u32[]{:S(2)}) async-start(s32[32,1,1]{2,1,0:T(1,128)} %copy.14), calls=%async_computation.1 | async-start | bytes 32768 | tf_op jit(solution)/shard_map/all_to_all | solution.py:536
  22.1 4.1 %copy-start.14 = (bf16[4,1408,64]{1,2,0:T(8,128)(2,1)S(1)}, bf16[4,1408,64]{1,2,0:T(8,128)(2,1)}, u32[]{:S(2)}) copy-start(bf16[4,1408,64]{1,2,0:T(8,128)(2,1)} %param.10) | copy-start | bytes 2162692
  22.1 4.1 %copy-start.16 = (f32[1408]{0:T(1024)S(1)}, f32[1408]{0:T(1024)}, u32[]{:S(2)}) copy-start(f32[1408]{0:T(1024)} %param.11) | copy-start | bytes 16900
  22.1 16.0 %all-to-all-start = ((bf16[8,2,176,128]{3,2,1,0:T(8,128)(2,1)}), bf16[8,2,176,128]{3,2,1,0:T(8,128)(2,1)S(1)}, u32[]{:S(2)}, u32[]{:S(2)}) async-start(bf16[8,2,176,128]{3,2,1,0:T(8,128)(2,1)} %pack_longest.1), calls=%async_computation | async-start | bytes 1441792 | tf_op jit(solution)/shard_map/all_to_all | solution.py:617
  38.1 0.9 copy-start.5
  38.9 16.6 %all-to-all-start.2 = ((bf16[32,4,1408]{2,1,0:T(4,128)(2,1)}), bf16[32,4,1408]{2,1,0:T(4,128)(2,1)S(1)}, u32[]{:S(2)}, u32[]{:S(2)}) async-start(bf16[32,4,1408]{2,1,0:T(4,128)(2,1)} %reshape.147), calls=%async_computation.2 | async-start | bytes 720896 | tf_op jit(solution)/shard_map/all_to_all | solution.py:535
  55.5 8.9 %copy-start.15 = (bf16[32,4,1408]{2,1,0:T(4,128)(2,1)}, bf16[32,4,1408]{2,1,0:T(4,128)(2,1)S(1)}, u32[]{:S(2)}) copy-start(bf16[32,4,1408]{2,1,0:T(4,128)(2,1)S(1)} %all-to-all-done.2) | copy-start | bytes 1081348
  55.5 37.8 %all-to-all-start.4 = ((bf16[32,176,128]{2,1,0:T(8,128)(2,1)}), bf16[32,176,128]{2,1,0:T(8,128)(2,1)S(1)}, u32[]{:S(2)}, u32[]{:S(2)}) async-start(bf16[32,176,128]{2,1,0:T(8,128)(2,1)} %pack_blocks.5), calls=%async_computation.4 | async-start | bytes 2883584 | tf_op jit(solution)/shard_map/all_to_all | solution.py:617
  93.3 38.4 %all-to-all-start.5 = ((bf16[32,176,128]{2,1,0:T(8,128)(2,1)}), bf16[32,176,128]{2,1,0:T(8,128)(2,1)S(1)}, u32[]{:S(2)}, u32[]{:S(2)}) async-start(bf16[32,176,128]{2,1,0:T(8,128)(2,1)} %pack_blocks.6), calls=%async_computation.5 | async-start | bytes 2883584 | tf_op jit(solution)/shard_map/all_to_all | solution.py:617
  107.1 2.2 copy-start.17
  131.8 54.3 %all-to-all-start.6 = ((bf16[32,176,128]{2,1,0:T(8,128)(2,1)}), bf16[32,176,128]{2,1,0:T(8,128)(2,1)}, u32[]{:S(2)}, u32[]{:S(2)}) async-start(bf16[32,176,128]{2,1,0:T(8,128)(2,1)} %pack_blocks.7), calls=%async_computation.6 | async-start | bytes 2883584 | tf_op jit(solution)/shard_map/all_to_all | solution.py:617
  135.5 1.4 copy-start
  149.1 1.1 copy-start.1
  151.1 2.5 collective-permute-start
  156.7 12.8 %collective-permute-start.1 = (bf16[2,176,512]{2,1,0:T(8,128)(2,1)S(1)}, bf16[2,176,512]{2,1,0:T(8,128)(2,1)}, u32[]{:S(2)}, u32[]{:S(2)}) collective-permute-start(bf16[2,176,512]{2,1,0:T(8,128)(2,1)S(1)} %dynamic-slice_bitcast_fusion.1), channel_id=1, source_target_pairs={{0,2},{1,3},{2,0},{3,1},{4,6},{5,7},{6,4},{7,5},{8,10},{9,11},{10,... | collective-permute-start | bytes 1081352 | tf_op jit(solution)/shard_map/ppermute | solution.py:567
  170.7 6.5 %collective-permute-start.2 = (bf16[1,176,512]{2,1,0:T(8,128)(2,1)S(1)}, bf16[1,176,512]{2,1,0:T(8,128)(2,1)}, u32[]{:S(2)}, u32[]{:S(2)}) collective-permute-start(bf16[1,176,512]{2,1,0:T(8,128)(2,1)S(1)} %constant_dynamic-slice_fusion.1), channel_id=1, source_target_pairs={{0,4},{1,5},{2,6},{3,7},{4,0},{5,1},{6,2},{7,3},{8,12},{9,13},{10,... | collective-permute-start | bytes 540680 | tf_op jit(solution)/shard_map/ppermute | solution.py:567
  178.2 12.2 %collective-permute-start.3 = (bf16[1,176,512]{2,1,0:T(8,128)(2,1)S(1)}, bf16[1,176,512]{2,1,0:T(8,128)(2,1)S(1)}, u32[]{:S(2)}, u32[]{:S(2)}) collective-permute-start(bf16[1,176,512]{2,1,0:T(8,128)(2,1)S(1)} %dynamic-slice_select_fusion), channel_id=1, source_target_pairs={{0,8},{1,9},{2,10},{3,11},{4,12},{5,13},{6,14},{7,15},{8,0},{9,1},... | collective-permute-start | bytes 540680 | tf_op jit(solution)/shard_map/ppermute | solution.py:567
  186.1 101.6 %all-to-all-start.3 = ((bf16[32,176,128]{2,1,0:T(8,128)(2,1)}), bf16[32,176,128]{2,1,0:T(8,128)(2,1)}, u32[]{:S(2)}, u32[]{:S(2)}) async-start(bf16[32,176,128]{2,1,0:T(8,128)(2,1)} %pack_blocks.4), calls=%async_computation.3 | async-start | bytes 2883584 | tf_op jit(solution)/shard_map/all_to_all | solution.py:617
  190.4 41.8 %collective-permute-start.4 = (bf16[1,176,512]{2,1,0:T(8,128)(2,1)S(1)}, bf16[1,176,512]{2,1,0:T(8,128)(2,1)S(1)}, u32[]{:S(2)}, u32[]{:S(2)}) collective-permute-start(bf16[1,176,512]{2,1,0:T(8,128)(2,1)S(1)} %broadcast_select_fusion), channel_id=1, source_target_pairs={{0,16},{1,17},{2,18},{3,19},{4,20},{5,21},{6,22},{7,23},{8,24},{9,... | collective-permute-start | bytes 540680 | tf_op jit(solution)/shard_map/ppermute | solution.py:567
  232.2 1.1 copy-start.6
  235.6 6.5 %collective-permute-start.5 = (bf16[192,512]{1,0:T(8,128)(2,1)S(1)}, bf16[192,512]{1,0:T(8,128)(2,1)S(1)}, u32[]{:S(2)}, u32[]{:S(2)}) collective-permute-start(bf16[192,512]{1,0:T(8,128)(2,1)S(1)} %attend_longest.1.first_ref), channel_id=1, source_target_pairs={{0,8},{1,9},{2,10},{3,11},{4,12},{5,13},{6,14},{7,15},{8,0},{9,1},... | collective-permute-start | bytes 589832 | tf_op jit(solution)/shard_map/ppermute | solution.py:567
  242.2 10.7 %collective-permute-start.6 = (bf16[192,512]{1,0:T(8,128)(2,1)S(1)}, bf16[192,512]{1,0:T(8,128)(2,1)S(1)}, u32[]{:S(2)}, u32[]{:S(2)}) collective-permute-start(bf16[192,512]{1,0:T(8,128)(2,1)S(1)} %fold_parts.2.first_ref), channel_id=1, source_target_pairs={{0,16},{1,17},{2,18},{3,19},{4,20},{5,21},{6,22},{7,23},{8,24},{9,... | collective-permute-start | bytes 589832 | tf_op jit(solution)/shard_map/ppermute | solution.py:567
  253.1 6.8 %collective-permute-start.7 = (bf16[1,192,512]{2,1,0:T(8,128)(2,1)S(1)}, bf16[1,192,512]{2,1,0:T(8,128)(2,1)S(1)}, u32[]{:S(2)}, u32[]{:S(2)}) collective-permute-start(bf16[1,192,512]{2,1,0:T(8,128)(2,1)S(1)} %bitcast.34), channel_id=1, source_target_pairs={{0,4},{1,5},{2,6},{3,7},{4,0},{5,1},{6,2},{7,3},{8,12},{9,13},{10,... | collective-permute-start | bytes 589832 | tf_op jit(solution)/shard_map/ppermute | solution.py:567
  260.7 10.5 %collective-permute-start.8 = (bf16[2,192,512]{2,1,0:T(8,128)(2,1)}, bf16[2,192,512]{2,1,0:T(8,128)(2,1)}, u32[]{:S(2)}, u32[]{:S(2)}) collective-permute-start(bf16[2,192,512]{2,1,0:T(8,128)(2,1)} %maximum_select_fusion.2), channel_id=1, source_target_pairs={{0,2},{1,3},{2,0},{3,1},{4,6},{5,7},{6,4},{7,5},{8,10},{9,11},{10,... | collective-permute-start | bytes 1179656 | tf_op jit(solution)/shard_map/ppermute | solution.py:567
  261.9 1.4 copy-start.2
  263.3 1.8 copy-start.11
  270.5 3.1 %copy-start.3 = (bf16[8,176,512]{2,1,0:T(8,128)(2,1)S(1)}, bf16[8,176,512]{2,1,0:T(8,128)(2,1)}, u32[]{:S(2)}) copy-start(bf16[8,176,512]{2,1,0:T(8,128)(2,1)} %copy-done.1) | copy-start | bytes 4325380
  273.5 6.4 %copy-start.12 = (bf16[2,1408,512]{2,1,0:T(8,128)(2,1)S(1)}, bf16[2,1408,512]{2,1,0:T(8,128)(2,1)}, u32[]{:S(2)}) copy-start(bf16[2,1408,512]{2,1,0:T(8,128)(2,1)} %get-tuple-element.4.own_ref) | copy-start | bytes 8650756
  273.5 22.3 %collective-permute-start.9 = (bf16[4,192,512]{2,1,0:T(8,128)(2,1)}, bf16[4,192,512]{2,1,0:T(8,128)(2,1)}, u32[]{:S(2)}, u32[]{:S(2)}) collective-permute-start(bf16[4,192,512]{2,1,0:T(8,128)(2,1)} %maximum_select_fusion.1), channel_id=1, source_target_pairs={{0,1},{1,0},{2,3},{3,2},{4,5},{5,4},{6,7},{7,6},{8,9},{9,8},{10,11... | collective-permute-start | bytes 2359304 | tf_op jit(solution)/shard_map/ppermute | solution.py:567
  279.2 0.7 copy-start.7
  280.0 7.7 %copy-start.13 = (bf16[2,1408,512]{2,1,0:T(8,128)(2,1)S(1)}, bf16[2,1408,512]{2,1,0:T(8,128)(2,1)}, u32[]{:S(2)}) copy-start(bf16[2,1408,512]{2,1,0:T(8,128)(2,1)} %get-tuple-element.4.own_ref) | copy-start | bytes 8650756
  286.9 0.7 copy-start.9
  287.7 1.4 copy-start.4
  295.8 2.2 copy-start.8
  295.8 2.2 copy-start.10

commit v2 on v1

--- a/solution.py
+++ b/solution.py
@@ -15,7 +15,7 @@
 EXT = PAIR + 16
 LANES = 128
 MASKED = -1e30
-VMEM = 48 * 1024 * 1024
+VMEM = 60 * 1024 * 1024
 
 
 masked_score = -1e30
@@ -219,46 +219,47 @@
             tile = cache_ref[g // 2, g % 2, :, pl.ds(start, LANES)]
             tile = pltpu.roll(tile, (g + 4 - turn) % 4 * BS, 1)
             packed = tile if g == 0 else jnp.where(lane == g, tile, packed)
-        out_ref[w] = packed
+        out_ref[w, 0] = packed
         return carry
 
-    lax.fori_loop(0, slots, one, 0, unroll=2)
-
-
-def pack_unit(ids, paged, unit):
+    lax.fori_loop(0, slots, one, 0, unroll=8)
+
+
+def pack_units(ids, paged, first, count):
     slots = ids.shape[0]
     lanes = paged.shape[3]
     return pl.pallas_call(
         functools.partial(pack_body, slots=slots),
         grid_spec=pltpu.PrefetchScalarGridSpec(
             num_scalar_prefetch=1,
-            grid=(1,),
-            in_specs=[pl.BlockSpec((2, 2, PAIR, lanes), lambda i, s: (0, unit, 0, 0))],
-            out_specs=pl.BlockSpec((slots, PAIR, LANES), lambda i, s: (0, 0, 0)),
-        ),
-        out_shape=jax.ShapeDtypeStruct((slots, PAIR, LANES), jnp.bfloat16),
+            grid=(count,),
+            in_specs=[pl.BlockSpec((2, 2, PAIR, lanes), lambda i, s: (0, first + i, 0, 0))],
+            out_specs=pl.BlockSpec((slots, 1, PAIR, LANES), lambda i, s: (0, i, 0, 0)),
+        ),
+        out_shape=jax.ShapeDtypeStruct((slots, count, PAIR, LANES), jnp.bfloat16),
         compiler_params=pltpu.CompilerParams(vmem_limit_bytes=VMEM),
-        cost_estimate=pl.CostEstimate(flops=0, bytes_accessed=4500000, transcendentals=0),
+        cost_estimate=pl.CostEstimate(
+            flops=0, bytes_accessed=4500000 * count, transcendentals=0
+        ),
         name="pack_blocks",
     )(ids, paged)
 
 
 def star_pack_body(ids, *refs):
-    out_ref = refs[8]
     lane = lax.broadcasted_iota(jnp.int32, (PAIR, LANES), 1) // BS
     for c in range(2):
         packed = None
         for j in range(4):
-            tile = pltpu.roll(refs[c * 4 + j][0, 0], (j + 4 - ids[j] % 4) % 4 * BS, 1)
+            tile = pltpu.roll(refs[c * 4 + j][0, 0], (j + 4 - ids[1 + j] % 4) % 4 * BS, 1)
             packed = tile if j == 0 else jnp.where(lane == j, tile, packed)
-        out_ref[0, c] = packed
+        refs[8][0, c] = packed
 
 
 def star_pack(ids, paged):
     pairs = paged.shape[1]
 
     def spec(c, j):
-        return pl.BlockSpec((1, 1, PAIR, LANES), lambda i, s: (c, pair_of(i), 0, s[j] // 4))
+        return pl.BlockSpec((1, 1, PAIR, LANES), lambda i, s: (c, i ^ s[0], 0, s[1 + j] // 4))
 
     return pl.pallas_call(
         star_pack_body,
@@ -270,59 +271,67 @@
         ),
         out_shape=jax.ShapeDtypeStruct((pairs, 2, PAIR, LANES), jnp.bfloat16),
         compiler_params=pltpu.CompilerParams(vmem_limit_bytes=VMEM),
+        cost_estimate=pl.CostEstimate(flops=0, bytes_accessed=4000000, transcendentals=0),
         name="pack_longest",
     )(ids, *([paged] * 8))
 
 
-def pair_of(place):
-    return place % 2 * 4 + place // 2 % 2 * 2 + place // 4
-
-
-def project_body(normed_ref, weight_ref, cos_ref, sin_ref, query_ref, cache_ref):
+def rotate_heads(x, cosine, sine):
+    heads = []
+    for h in range(2):
+        one = x[h * HD : (h + 1) * HD]
+        other = jnp.concatenate([one[HD // 2 :], one[: HD // 2]], axis=0)
+        heads.append(one * cosine + other * sine)
+    return jnp.concatenate(heads, axis=0).astype(jnp.bfloat16)
+
+
+def query_body(normed_ref, weight_ref, cos_ref, sin_ref, query_ref):
+    x = jnp.dot(weight_ref[0], normed_ref[...], preferred_element_type=jnp.float32)
+    for g in range(query_ref.shape[0]):
+        query_ref[g] = rotate_heads(x[g * PAIR : (g + 1) * PAIR], cos_ref[...], sin_ref[...])
+
+
+def cache_body(normed_ref, key_ref, value_ref, cos_ref, sin_ref, cache_ref):
     normed = normed_ref[...]
-
-    def part(j):
-        return jnp.dot(weight_ref[j], normed, preferred_element_type=jnp.float32)
-
-    def rotate(x):
-        heads = []
-        for h in range(2):
-            one = x[h * HD : (h + 1) * HD]
-            other = jnp.concatenate([one[HD // 2 :], one[: HD // 2]], axis=0)
-            heads.append(one * cos_ref[...] + other * sin_ref[...])
-        return jnp.concatenate(heads, axis=0).astype(jnp.bfloat16)
-
-    query_ref[0] = rotate(part(0))
-    cache_ref[0] = rotate(part(1))
-    cache_ref[1] = part(2).astype(jnp.bfloat16)
-
-
-def project(normed, wqkv, cosine, sine):
+    x = jnp.dot(key_ref[0], normed, preferred_element_type=jnp.float32)
+    for g in range(x.shape[0] // PAIR):
+        span = slice(g * PAIR, (g + 1) * PAIR)
+        cache_ref[0, span] = rotate_heads(x[span], cos_ref[...], sin_ref[...])
+    x = jnp.dot(value_ref[0], normed, preferred_element_type=jnp.float32)
+    cache_ref[1] = x.astype(jnp.bfloat16)
+
+
+def project(normed, wqkv, cosine, sine, parts):
     width, rows = normed.shape
     pairs = width // PAIR
+    table = pl.BlockSpec((HD, rows), lambda i: (0, 0))
+    query = len(parts) == 1
+
+    def weight(j):
+        return pl.BlockSpec((1, 2 * PAIR, width), lambda i: (j, i, 0))
+
+    if query:
+        out_spec = pl.BlockSpec((2, PAIR, rows), lambda i: (i, 0, 0))
+        out_shape = jax.ShapeDtypeStruct((pairs, PAIR, rows), jnp.bfloat16)
+    else:
+        out_spec = pl.BlockSpec((2, 2 * PAIR, rows), lambda i: (0, i, 0))
+        out_shape = jax.ShapeDtypeStruct((2, width, rows), jnp.bfloat16)
     return pl.pallas_call(
-        project_body,
-        grid=(pairs,),
-        in_specs=[
-            pl.BlockSpec((width, rows), lambda i: (0, 0)),
-            pl.BlockSpec((3, PAIR, width), lambda i: (0, i, 0)),
-            pl.BlockSpec((HD, rows), lambda i: (0, 0)),
-            pl.BlockSpec((HD, rows), lambda i: (0, 0)),
-        ],
-        out_specs=[
-            pl.BlockSpec((1, PAIR, rows), lambda i: (i, 0, 0)),
-            pl.BlockSpec((2, PAIR, rows), lambda i: (0, i, 0)),
-        ],
-        out_shape=[
-            jax.ShapeDtypeStruct((pairs, PAIR, rows), jnp.bfloat16),
-            jax.ShapeDtypeStruct((2, width, rows), jnp.bfloat16),
-        ],
+        query_body if query else cache_body,
+        grid=(pairs // 2,),
+        in_specs=[pl.BlockSpec((width, rows), lambda i: (0, 0))]
+        + [weight(j) for j in parts]
+        + [table, table],
+        out_specs=out_spec,
+        out_shape=out_shape,
         compiler_params=pltpu.CompilerParams(vmem_limit_bytes=VMEM),
         cost_estimate=pl.CostEstimate(
-            flops=6 * width * width * rows, bytes_accessed=8 * width * width, transcendentals=0
-        ),
-        name="project_rotate",
-    )(normed, wqkv, cosine, sine)
+            flops=2 * len(parts) * width * width * rows,
+            bytes_accessed=3 * len(parts) * width * width,
+            transcendentals=0,
+        ),
+        name="project_query" if query else "project_cache",
+    )(normed, *([wqkv] * len(parts)), cosine, sine)
 
 
 def split_three(x):
@@ -374,7 +383,7 @@
         kv[g, 0:PAIR, old:] = own_ref[0, g * PAIR : (g + 1) * PAIR]
         kv[2 + g, 0:PAIR, old:] = own_ref[1, g * PAIR : (g + 1) * PAIR]
     for t in range(old // LANES):
-        tiles = [arrived_ref[4 * t + j] for j in range(4)]
+        tiles = [arrived_ref[4 * t + j, 0] for j in range(4)]
         for g in range(4):
             kv[g, 0:PAIR, t * LANES : (t + 1) * LANES] = jnp.concatenate(
                 [tile[:, g * BS : (g + 1) * BS] for tile in tiles], axis=1
@@ -383,7 +392,7 @@
         attend_pair(query_ref[g], kv.at[g], kv.at[2 + g], old, True, out_ref.at[g])
 
 
-def attend_unit(arrived, bias, queries, new_cache, unit):
+def attend_unit(arrived, place, bias, queries, new_cache, unit):
     rows = queries.shape[2]
     old = bias.shape[1]
     work = 4 * rows * (old + rows)
@@ -391,7 +400,7 @@
         functools.partial(attend_body, own_rows=rows),
         grid=(1,),
         in_specs=[
-            pl.BlockSpec(arrived.shape, lambda i: (0, 0, 0)),
+            pl.BlockSpec((arrived.shape[0], 1, PAIR, LANES), lambda i: (0, place, 0, 0)),
             pl.BlockSpec((1, old), lambda i: (0, 0)),
             pl.BlockSpec((2, PAIR, rows), lambda i: (unit, 0, 0)),
             pl.BlockSpec((2, 2 * PAIR, rows), lambda i: (0, unit, 0)),
@@ -399,7 +408,7 @@
         out_specs=pl.BlockSpec((2, EXT, rows), lambda i: (0, 0, 0)),
         out_shape=jax.ShapeDtypeStruct((2, EXT, rows), jnp.bfloat16),
         scratch_shapes=[pltpu.VMEM((4, EXT, old + rows), jnp.bfloat16)],
-        compiler_params=pltpu.CompilerParams(vmem_limit_bytes=VMEM),
+        compiler_params=pltpu.CompilerParams(vmem_limit_bytes=VMEM // 2),
         cost_estimate=pl.CostEstimate(
             flops=work * 1024, bytes_accessed=4000000, transcendentals=work
         ),
@@ -407,19 +416,20 @@
     )(arrived, bias, queries, new_cache)
 
 
-def star_body(arrived_ref, query_ref, out_ref, kv, *, sources):
+def star_body(*refs, sources):
+    query_ref, out_ref, kv = refs[sources:]
     lower = lax.broadcasted_iota(jnp.int32, (EXT - PAIR, sources * LANES), 0)
     kv[0, PAIR:EXT] = jnp.zeros(lower.shape, jnp.bfloat16)
     kv[1, PAIR:EXT] = jnp.where(lower == 0, 1.0, 0.0).astype(jnp.bfloat16)
     for s in range(sources):
         for c in range(2):
-            kv[c, 0:PAIR, s * LANES : (s + 1) * LANES] = arrived_ref[s, c]
-    attend_pair(query_ref[...], kv.at[0], kv.at[1], sources * LANES, False, out_ref)
+            kv[c, 0:PAIR, s * LANES : (s + 1) * LANES] = refs[s][0, c]
+    attend_pair(query_ref[0], kv.at[0], kv.at[1], sources * LANES, False, out_ref)
 
 
 def star_attend(arrived, query):
-    sources = arrived.shape[0]
-    rows = query.shape[1]
+    sources = len(arrived)
+    rows = query.shape[2]
     work = 2 * rows * sources * LANES
     return pl.pallas_call(
         functools.partial(star_body, sources=sources),
@@ -430,7 +440,7 @@
             flops=work * 1024, bytes_accessed=1500000, transcendentals=work
         ),
         name="attend_longest",
-    )(arrived, query)
+    )(*arrived, query)
 
 
 def fold_two(first, second):
@@ -468,78 +478,121 @@
     )(first, second)
 
 
-def finish_body(flag, star_ref, *refs):
-    out_ref = refs[-1]
-    for u, unit_ref in enumerate(refs[:-1]):
-        for g in range(2):
-            pair = 2 * u + g
-            span = pl.ds(pair * PAIR, PAIR)
-            out_ref[span] = unit_ref[g, 0:PAIR]
-
-            @pl.when(flag[0] == 1)
-            def _():
-                heads, _ = fold_two(unit_ref[g].astype(jnp.float32), star_ref[pair].astype(jnp.float32))
-                out_ref[span] = jnp.concatenate(heads, axis=0).astype(jnp.bfloat16)
-
-
-def finish(flag, star, units):
-    pairs, _, rows = star.shape
-    whole = [pl.BlockSpec(star.shape, lambda i, s: (0, 0, 0))]
+def finish_body(scalars, own_ref, other_ref, *refs):
+    units, out_ref, held = refs[:-2], refs[-2], refs[-1]
+    pairs = held.shape[0]
+    for i in range(pairs):
+        out_ref[i * PAIR : (i + 1) * PAIR] = units[i // 2][i % 2, 0:PAIR]
+
+    @pl.when(scalars[0] == 1)
+    def _():
+        for i in range(pairs):
+            held[i] = units[i // 2][i % 2]
+        for i in range(pairs):
+            pair = scalars[1] ^ i
+            star = own_ref[i] if i < pairs // 2 else other_ref[i - pairs // 2]
+            heads, _ = fold_two(held[pair].astype(jnp.float32), star.astype(jnp.float32))
+            span = pl.ds(pl.multiple_of(pair * PAIR, 16), PAIR)
+            out_ref[span] = jnp.concatenate(heads, axis=0).astype(jnp.bfloat16)
+
+
+def finish(scalars, own, other, units):
+    pairs = 2 * own.shape[0]
+    rows = own.shape[2]
     return pl.pallas_call(
         finish_body,
         grid_spec=pltpu.PrefetchScalarGridSpec(
             num_scalar_prefetch=1,
             grid=(1,),
-            in_specs=whole + [pl.BlockSpec(u.shape, lambda i, s: (0, 0, 0)) for u in units],
+            in_specs=[pl.BlockSpec(x.shape, lambda i, s: (0, 0, 0)) for x in [own, other] + units],
             out_specs=pl.BlockSpec((pairs * PAIR, rows), lambda i, s: (0, 0)),
+            scratch_shapes=[pltpu.VMEM((pairs, EXT, rows), jnp.bfloat16)],
         ),
         out_shape=jax.ShapeDtypeStruct((pairs * PAIR, rows), jnp.bfloat16),
         compiler_params=pltpu.CompilerParams(vmem_limit_bytes=VMEM),
         name="finish_heads",
-    )(flag, star, *units)
-
-
-def place_and_norm(vision, ln_gain, merge_proj, image_slot, text, rms_gain):
-    groups = vision.shape[2]
-    width = vision.shape[1]
-    floats = vision.astype(jnp.float32)
-    average = jnp.sum(floats, axis=1) / D
-    spread = jnp.sum(floats * floats, axis=1) / D - average * average
-    normed_vision = (
-        (floats - average[:, None, :])
-        * lax.rsqrt(spread + 1e-06)[:, None, :]
-        * ln_gain[None, :, None]
-    ).astype(jnp.bfloat16)
-    merged = jnp.einsum(
-        "tcd,tcg->gd", merge_proj, normed_vision, preferred_element_type=jnp.float32
-    ).astype(jnp.bfloat16)
+    )(scalars, own, other, *units)
+
+
+def merge_body(slots, vision_ref, gain_ref, weight_ref, out_ref, total, *, rows_here, width):
+    step = pl.program_id(0)
+    floats = vision_ref[0].astype(jnp.float32)
+    average = jnp.sum(floats, axis=1, keepdims=True) / D
+    spread = jnp.sum(floats * floats, axis=1, keepdims=True) / D - average * average
+    normed = ((floats - average) * lax.rsqrt(spread + 1e-06) * gain_ref[...]).astype(jnp.bfloat16)
+    product = jnp.dot(normed, weight_ref[0], preferred_element_type=jnp.float32)
+
+    @pl.when(step == 0)
+    def _():
+        total[...] = product
+
+    @pl.when(step > 0)
+    def _():
+        total[...] += product
+
+    @pl.when(step == pl.num_programs(0) - 1)
+    def _():
+        devices, piece_rows = out_ref.shape[:2]
+        groups = total.shape[0]
+        pieces = groups // piece_rows
+        shape = (devices * piece_rows, groups)
+        row = lax.broadcasted_iota(jnp.int32, shape, 0)
+        column = lax.broadcasted_iota(jnp.int32, shape, 1)
+        label_row = lax.broadcasted_iota(jnp.int32, (groups, LANES), 0) // piece_rows
+        target = jnp.zeros(shape, jnp.int32)
+        label = jnp.zeros(label_row.shape, jnp.float32)
+        for j in range(pieces):
+            target = jnp.where(column // piece_rows == j, slots[j] // rows_here, target)
+            place = (slots[j] % rows_here // piece_rows + 1).astype(jnp.float32)
+            label = jnp.where(label_row == j, place, label)
+        hit = (target == row // piece_rows) & (column % piece_rows == row % piece_rows)
+        select = jnp.where(hit, 1.0, 0.0).astype(jnp.bfloat16)
+        wide = jnp.concatenate([total[...].astype(jnp.bfloat16), label.astype(jnp.bfloat16)], axis=1)
+        sent = jnp.dot(select, wide, preferred_element_type=jnp.float32).astype(jnp.bfloat16)
+        for w in range(devices):
+            out_ref[w] = sent[w * piece_rows : (w + 1) * piece_rows]
+
+
+def merge_rows(vision, ln_gain, merge_proj, image_slot, rows_here):
+    parts, width, groups = vision.shape
     devices = lax.axis_size("blk")
-    rows_here = text.shape[1]
-    pieces = image_slot.shape[0]
-    piece_rows = groups // pieces
+    piece_rows = groups // image_slot.shape[0]
+    return pl.pallas_call(
+        functools.partial(merge_body, rows_here=rows_here, width=width),
+        grid_spec=pltpu.PrefetchScalarGridSpec(
+            num_scalar_prefetch=1,
+            grid=(parts,),
+            in_specs=[
+                pl.BlockSpec((1, groups, width), lambda i, s: (i, 0, 0)),
+                pl.BlockSpec((1, width), lambda i, s: (0, 0)),
+                pl.BlockSpec((1, width, width), lambda i, s: (i, 0, 0)),
+            ],
+            out_specs=pl.BlockSpec((devices, piece_rows, width + LANES), lambda i, s: (0, 0, 0)),
+            scratch_shapes=[pltpu.VMEM((groups, width), jnp.float32)],
+        ),
+        out_shape=jax.ShapeDtypeStruct((devices, piece_rows, width + LANES), jnp.bfloat16),
+        compiler_params=pltpu.CompilerParams(vmem_limit_bytes=VMEM),
+        cost_estimate=pl.CostEstimate(
+            flops=2 * groups * parts * width * width,
+            bytes_accessed=2 * parts * width * width,
+            transcendentals=0,
+        ),
+        name="merge_pieces",
+    )(image_slot, jnp.transpose(vision, (0, 2, 1)), ln_gain.reshape(1, width), merge_proj)
+
+
+def place_and_norm(arrived, text, rms_gain):
+    width, rows_here = text.shape
+    devices, piece_rows = arrived.shape[:2]
     lines = jnp.arange(rows_here, dtype=jnp.int32)
     offsets = jnp.arange(piece_rows, dtype=jnp.int32)
-    target = image_slot // rows_here
-    within = image_slot % rows_here
-    select = target[None, :] == jnp.arange(devices, dtype=jnp.int32)[:, None]
-    outbound = (
-        jnp.dot(
-            select.astype(jnp.bfloat16),
-            merged.reshape(pieces, piece_rows * width),
-            preferred_element_type=jnp.float32,
-        )
-        .astype(jnp.bfloat16)
-        .reshape(devices, piece_rows, width)
-    )
-    starts = jnp.sum(jnp.where(select, within[None, :] + 1, 0), axis=1) - 1
-    arrived = lax.all_to_all(outbound, "blk", split_axis=0, concat_axis=0, tiled=True)
-    arrived_start = lax.all_to_all(starts, "blk", split_axis=0, concat_axis=0, tiled=True)
-    row_ids = (arrived_start[:, None] + offsets[None, :]).reshape(-1)
-    present = jnp.repeat(arrived_start >= 0, piece_rows)
+    starts = (arrived[:, 0, width].astype(jnp.int32) - 1) * piece_rows
+    row_ids = (starts[:, None] + offsets[None, :]).reshape(-1)
+    present = jnp.repeat(starts >= 0, piece_rows)
     hits = (row_ids[:, None] == lines[None, :]) & present[:, None]
     placed_rows = jnp.einsum(
         "kl,kr->lr",
-        arrived.reshape(devices * piece_rows, width),
+        arrived[:, :, :width].reshape(devices * piece_rows, width),
         hits.astype(jnp.bfloat16),
         preferred_element_type=jnp.float32,
     ).astype(jnp.bfloat16)
@@ -578,6 +631,9 @@
     table_width = block_table.shape[1]
     each = table_width // devices
 
+    tie = lax.optimization_barrier
+    outbound = merge_rows(vision, ln_gain, merge_proj, image_slot, rows)
+    outbound, block_table = tie((outbound, block_table))
     holder = jnp.where(block_table >= 0, block_table // owned, -1)
     local = block_table - here * owned
     mine = holder == here
@@ -611,46 +667,88 @@
 
     paged = pcache.reshape(2, pairs, PAIR, owned * BS)
     units = pairs // 2
-    planes = [[p * pairs + i for i in range(pairs)] for p in range(devices // pairs)]
-
-    def exchange(x, groups=None):
-        return lax.all_to_all(x, "blk", split_axis=0, concat_axis=0, tiled=True, axis_index_groups=groups)
-
-    arrived = []
-    for u in range(units):
-        arrived.append(exchange(pack_unit(chosen, paged, u)))
-    star_kv = exchange(star_pack(star_ids, paged), planes)
-
-    normed = place_and_norm(vision, ln_gain, merge_proj, image_slot, text, rms_gain)
+
+    def exchange(x):
+        return lax.all_to_all(x, "blk", split_axis=0, concat_axis=0, tiled=True)
+
+    pieces_in = exchange(outbound)
+    head = units - 1
+    packed = pack_units(chosen, paged, 0, head)
+    packed, pieces_in = tie((packed, pieces_in))
+    arrived = exchange(packed)
+    packed_last = pack_units(chosen, paged, head, units - head)
+
+    normed = place_and_norm(pieces_in, text, rms_gain)
+    normed, packed_last = tie((normed, packed_last))
     places = (cache_len[0] + jnp.arange(rows, dtype=jnp.int32)).astype(jnp.float32)
-    queries, new_cache = project(normed, wqkv, *rotary_tables(places))
-
-    query = queries
+    tables = rotary_tables(places)
+    queries = project(normed, wqkv, *tables, (0,))
+
     plane_bits = pairs.bit_length() - 1
     all_bits = devices.bit_length() - 1
+    place = here % pairs
+    pair = place % 2 * 4 + place // 2 % 2 * 2 + place // 4
+    query = queries
     for bit in range(plane_bits):
         mine_bit, star_bit = (here >> bit) & 1, (longest >> bit) & 1
         halves = query.reshape(2, query.shape[0] // 2, PAIR, rows)
         kept = lax.dynamic_index_in_dim(halves, mine_bit, 0, False)
         given = lax.dynamic_index_in_dim(halves, 1 - mine_bit, 0, False)
-        query = jnp.where(star_bit == mine_bit, kept, swap(given, bit))
+        taken = swap(given, bit)
+        if bit == 0:
+            normed, taken = tie((normed, taken))
+            new_cache = project(normed, wqkv, *tables, (1, 2))
+        if bit == 1:
+            taken, new_cache = tie((taken, new_cache))
+            star_ids, taken = tie((star_ids, taken))
+            star_ids = jnp.concatenate([pair.astype(jnp.int32).reshape(1), star_ids])
+            star_kv = star_pack(star_ids, paged)
+        if bit == 2:
+            taken, star_kv = tie((taken, star_kv))
+            star_parts = [star_kv[0:1]]
+            for i in range(1, pairs):
+                away = i % 2 * 4 + i // 2 % 2 * 2 + i // 4
+                star_parts.append(
+                    lax.ppermute(star_kv[i : i + 1], "blk", [(d, d ^ away) for d in range(devices)])
+                )
+        query = jnp.where(star_bit == mine_bit, kept, taken)
     for bit in range(plane_bits, all_bits):
         same = ((here ^ longest) >> bit) & 1
         query = jnp.where(same == 0, query, swap(query, bit))
-    star = star_attend(star_kv, query[0])
+    star_parts, query = tie((star_parts, query))
+    star = star_attend(star_parts, query)
+    results = []
+    came = [arrived]
+
+    def attend_next(*after):
+        u = len(results)
+        held, *_ = tie((bias, *after))
+        chunk, place = (came[0], u) if u < head else (came[1], u - head)
+        results.append(attend_unit(chunk, place, held, queries, new_cache, u))
+
+    half = pairs // 2
+    mates = [i % 2 * 4 + i // 2 % 2 * 2 + i // 4 for i in range(half)]
     for bit in range(plane_bits, all_bits):
-        star = fold(star, swap(star, bit))
-    star = star[None]
-    for bit in reversed(range(plane_bits)):
         other = swap(star, bit)
-        mine_bit = (here >> bit) & 1
-        star = jnp.where(
-            mine_bit == 0, jnp.concatenate([star, other]), jnp.concatenate([other, star])
-        )
-
-    results = [attend_unit(arrived[u], bias, queries, new_cache, u) for u in range(units)]
-    flag = (here == longest).astype(jnp.int32).reshape(1)
-    return (finish(flag, star, results), new_cache)
+        if bit == all_bits - 1:
+            attend_next(star)
+            other, results = tie((other, results))
+            packed_last, came[0], other = tie((packed_last, came[0], other))
+            came.append(exchange(packed_last))
+        star = fold(star, other)
+    own = [star]
+    for away in mates[1:]:
+        own.append(lax.ppermute(star, "blk", [(d, d ^ away) for d in range(devices)]))
+    while len(results) < head:
+        attend_next(star)
+    own, results = tie((own, results))
+    own = jnp.stack(own)
+    other = swap(own, 0)
+    while len(results) < units:
+        attend_next(own)
+    other, results = tie((other, results))
+    scalars = jnp.stack([(here == longest).astype(jnp.int32), pair.astype(jnp.int32)])
+    return (finish(scalars, own, other, results), new_cache)
 
 
 def spreads(mesh):

time: 301 us -> 221 us (0.73)
  waiting for transfers between devices: 136 us -> 60.4 us
  Pallas kernels: 72 us -> 84.3 us
  matrix products: 10.9 us -> 0.7 us
  other arithmetic: 16.5 us -> 9.62 us
  starting transfers between devices: 39.8 us -> 43.3 us
    all_to_all x7 -> x3, waiting for transfers between devices: 58.5 us -> 10.4 us  [exchange(): return lax.all_to_all(x, 'blk', split_axis=0, concat_axis=0, tiled=True)]
    ppermute x10 -> x8, waiting for transfers between devices: 77.6 us -> 43.4 us  [swap(): return lax.ppermute(x, 'blk', [(i, i ^ 1 << bit) for i in range(size)])]
    all_to_all x7 -> x3, starting transfers between devices: 28.8 us -> 15.2 us  [exchange(): return lax.all_to_all(x, 'blk', split_axis=0, concat_axis=0, tiled=True)]
    dot_general x3 -> x1, matrix products: 10.9 us -> 0.7 us  [place_and_norm(): jnp.einsum('kl,kr->lr', arrived[:, :, :width].reshape(devices * piece_row...]
    ppermute x0 -> x10, starting transfers between devices: none -> 9.28 us  [the longest x7 5.79 us: spread_shards(): lax.ppermute(star_kv[i:i + 1], 'blk', [(d, d ^ away) for d in range(devic...]
    select_n x6 -> x3, other arithmetic: 9.44 us -> 1.26 us  [spread_shards(): query = jnp.where(star_bit == mine_bit, kept, taken)]
    ppermute x10 -> x8, starting transfers between devices: 11 us -> 18.8 us  [swap(): return lax.ppermute(x, 'blk', [(i, i ^ 1 << bit) for i in range(size)])]
    ppermute x0 -> x10, waiting for transfers between devices: none -> 6.55 us  [the longest x3 3.71 us: spread_shards(): lax.ppermute(star, 'blk', [(d, d ^ away) for d in range(devices)])]
  transfers between devices with their start and end apart: 17 -> 21, of which waited for: 12 -> 8; matrix products, arithmetic and copies ran while one was open for 10% -> 6% of each run, Pallas kernels for 24% -> 32%
where the time goes in v2:
time: 221 us; the launch traced here: 219 us
  Pallas kernels  84.3 us (38%)
  waiting for transfers between devices  60.4 us (27%)
  starting transfers between devices  43.3 us (20%)
  local copies, waits for them, and re-layouts  14.2 us (6%)
  other arithmetic  9.62 us (4%)
  between operations  6.78 us (3%)
    ppermute x8, waiting for transfers between devices, swap(): return lax.ppermute(x, 'blk', [(i, i ^ 1 << bit) for i in range(size)])  43.4 us
    pallas_call x4, Pallas kernels, attend_unit(): pl.pallas_call(functools.partial(attend_body, own_rows=rows), grid=(1,),...  26.3 us
    ppermute x8, starting transfers between devices, swap(): return lax.ppermute(x, 'blk', [(i, i ^ 1 << bit) for i in range(size)])  18.8 us
    all_to_all x3, starting transfers between devices, exchange(): return lax.all_to_all(x, 'blk', split_axis=0, concat_axis=0, tiled=True)  15.2 us
    pallas_call x2, Pallas kernels, pack_units(): pl.pallas_call(functools.partial(pack_body, slots=slots), grid_spec=pltpu...  15.1 us
    pallas_call x2, Pallas kernels, project(): pl.pallas_call(query_body if query else cache_body, grid=(pairs // 2,), i...  15 us
    all_to_all x3, waiting for transfers between devices, exchange(): return lax.all_to_all(x, 'blk', split_axis=0, concat_axis=0, tiled=True)  10.4 us
    pallas_call x1, Pallas kernels, merge_rows(): pl.pallas_call(functools.partial(merge_body, rows_here=rows_here, width=w...  9.61 us
  transfers between devices with their start and end apart: 21, of which 8 were waited for; matrix products, arithmetic and copies ran while one was open for 6% of the time, Pallas kernels for 32%

profile of v2, /device:TPU:0, one launch (start us, length us, event | category | flops | bytes accessed | tf_op | source)
XLA Modules:
  0.0 219.2 jit_solution(17911986753601764322)
XLA Ops:
  0.6 1.3 reshape.119.gain_ref
  1.9 9.6 %merge_pieces.1 = bf16[32,4,1536]{2,1,0:T(4,128)(2,1)} custom-call(s32[16]{0:T(128)} %slots.1, bf16[4,64,1408]{2,1,0:T(8,128)(2,1)} %bitcast.42, f32[1,1408]{1,0:T(1,128)} %reshape.119.gain_ref, bf16[4,1408,1408]{2,1,0:T(8,128)(2,1)} %weight_ref.2), custom_call_target="tpu_custom_call" | custom-call | flops 1015021568 | bytes 15859712 | tf_op jit(solution)/shard_map/merge_pieces/pallas_call | solution.py:560
  11.5 7.3 %all-to-all-start = ((bf16[32,4,1536]{2,1,0:T(4,128)(2,1)}), bf16[32,4,1536]{2,1,0:T(4,128)(2,1)S(1)}, u32[]{:S(2)}, u32[]{:S(2)}) async-start(bf16[32,4,1536]{2,1,0:T(4,128)(2,1)} %merge_pieces.1), calls=%async_computation | async-start | bytes 786432 | tf_op jit(solution)/shard_map/all_to_all | solution.py:672
  19.5 9.6 %pack_blocks.2 = bf16[32,3,176,128]{3,2,1,0:T(8,128)(2,1)} custom-call(s32[32]{0:T(128)} %get-tuple-element.90.ids, bf16[2,8,176,2048]{3,2,1,0:T(8,128)(2,1)} %bitcast.29), custom_call_target="tpu_custom_call" | custom-call | bytes 13500000 | tf_op jit(solution)/shard_map/pack_blocks/pallas_call | solution.py:231
  29.1 3.0 %all-to-all-done = bf16[32,4,1536]{2,1,0:T(4,128)(2,1)S(1)} async-done(((bf16[32,4,1536]{2,1,0:T(4,128)(2,1)}), bf16[32,4,1536]{2,1,0:T(4,128)(2,1)S(1)}, u32[]{:S(2)}, u32[]{:S(2)}) %all-to-all-start) | async-done | bytes 393248 | tf_op jit(solution)/shard_map/all_to_all | solution.py:672
  32.0 3.6 %all-to-all-start.1 = ((bf16[32,3,176,128]{3,2,1,0:T(8,128)(2,1)}), bf16[32,3,176,128]{3,2,1,0:T(8,128)(2,1)}, u32[]{:S(2)}, u32[]{:S(2)}) async-start(bf16[32,3,176,128]{3,2,1,0:T(8,128)(2,1)} %pack_blocks.2), calls=%async_computation.1 | async-start | bytes 8650752 | tf_op jit(solution)/shard_map/all_to_all | solution.py:672
  35.7 5.6 %pack_blocks.3 = bf16[32,1,176,128]{3,2,1,0:T(8,128)(2,1)} custom-call(s32[32]{0:T(128)} %get-tuple-element.90.ids, bf16[2,8,176,2048]{3,2,1,0:T(8,128)(2,1)} %bitcast.30), custom_call_target="tpu_custom_call" | custom-call | bytes 4500000 | tf_op jit(solution)/shard_map/pack_blocks/pallas_call | solution.py:231
  42.5 0.8 pad_maximum_fusion.1
  45.4 1.5 fusion.2.normed_ref
  46.9 6.2 %project_query.1.query_ref = bf16[8,176,512]{2,1,0:T(8,128)(2,1)} custom-call(bf16[1408,512]{1,0:T(8,128)(2,1)} %fusion.2.normed_ref, bf16[3,1408,1408]{2,1,0:T(8,128)(2,1)} %value_ref.1, f32[88,512]{1,0:T(8,128)} %get-tuple-element.109.cos_ref, f32[88,512]{1,0:T(8,128)} %get-tuple-element.110.sin_ref), custom_call_target="tpu_custom_call" | custom-call | flops 2030043136 | bytes 5947392 | tf_op jit(solution)/shard_map/project_query/pallas_call | solution.py:319
  53.2 1.2 dynamic-slice_bitcast_fusion
  60.5 1.2 bitcast_select_fusion
  61.8 1.8 collective-permute-start.1
  63.5 8.8 %project_cache.1.own_ref = bf16[2,1408,512]{2,1,0:T(8,128)(2,1)} custom-call(bf16[1408,512]{1,0:T(8,128)(2,1)} %fusion.2.normed_ref, bf16[3,1408,1408]{2,1,0:T(8,128)(2,1)} %value_ref.1, bf16[3,1408,1408]{2,1,0:T(8,128)(2,1)} %value_ref.1, f32[88,512]{1,0:T(8,128)} %get-tuple-element.109.cos_ref, f32[88,512]{1,0:T(8,128)} %get-tuple-element.110.sin_ref), custom_call_target="tpu_custom_call" | custom-call | flops 4060086272 | bytes 11894784 | tf_op jit(solution)/shard_map/project_cache/pallas_call | solution.py:319
  72.3 3.6 %collective-permute-done.1 = bf16[2,176,512]{2,1,0:T(8,128)(2,1)S(1)} collective-permute-done((bf16[2,176,512]{2,1,0:T(8,128)(2,1)S(1)}, bf16[2,176,512]{2,1,0:T(8,128)(2,1)S(1)}, u32[]{:S(2)}, u32[]{:S(2)}) %collective-permute-start.1) | collective-permute-done | bytes 360480 | tf_op jit(solution)/shard_map/ppermute | solution.py:620
  76.0 11.7 %collective-permute-start.2 = (bf16[1,176,512]{2,1,0:T(8,128)(2,1)S(1)}, bf16[1,176,512]{2,1,0:T(8,128)(2,1)S(1)}, u32[]{:S(2)}, u32[]{:S(2)}) collective-permute-start(bf16[1,176,512]{2,1,0:T(8,128)(2,1)S(1)} %constant_dynamic-slice_fusion.1), channel_id=1, source_target_pairs={{0,4},{1,5},{2,6},{3,7},{4,0},{5,1},{6,2},{7,3},{8,12},{9,13},{10,... | collective-permute-start | bytes 540680 | tf_op jit(solution)/shard_map/ppermute | solution.py:620
  88.4 6.7 %pack_longest.1 = bf16[8,2,176,128]{3,2,1,0:T(8,128)(2,1)} custom-call(s32[5]{0:T(128)} %pad_add_fusion.1.ids, bf16[2,8,176,2048]{3,2,1,0:T(8,128)(2,1)} %bitcast.31, bf16[2,8,176,2048]{3,2,1,0:T(8,128)(2,1)} %bitcast.32, bf16[2,8,176,2048]{3,2,1,0:T(8,128)(2,1)} %bitcast.33, bf16[2,8,176,2048]{3,2,1,0:T(8,128)(2,1)} %bitcast.34, ...), custom_call_target="tpu_custom_call" | custom-call | bytes 4000000 | tf_op jit(solution)/shard_map/pack_longest/pallas_call | solution.py:264
  95.2 1.9 fusion.19
  97.1 1.2 collective-permute-start.8
  98.3 12.3 %collective-permute-done.10 = bf16[1,176,512]{2,1,0:T(8,128)(2,1)S(1)} collective-permute-done((bf16[1,176,512]{2,1,0:T(8,128)(2,1)S(1)}, bf16[1,176,512]{2,1,0:T(8,128)(2,1)S(1)}, u32[]{:S(2)}, u32[]{:S(2)}) %collective-permute-start.10) | collective-permute-done | bytes 180256 | tf_op jit(solution)/shard_map/ppermute | solution.py:620
  110.6 4.2 %collective-permute-start.11 = (bf16[1,176,512]{2,1,0:T(8,128)(2,1)S(1)}, bf16[1,176,512]{2,1,0:T(8,128)(2,1)S(1)}, u32[]{:S(2)}, u32[]{:S(2)}) collective-permute-start(bf16[1,176,512]{2,1,0:T(8,128)(2,1)S(1)} %broadcast_select_fusion), channel_id=1, source_target_pairs={{0,16},{1,17},{2,18},{3,19},{4,20},{5,21},{6,22},{7,23},{8,24},{9,... | collective-permute-start | bytes 540680 | tf_op jit(solution)/shard_map/ppermute | solution.py:620
  115.5 1.2 collective-permute-start.6
  116.6 0.9 collective-permute-start.5
  117.5 0.9 collective-permute-start.4
  118.4 21.8 %collective-permute-done.11 = bf16[1,176,512]{2,1,0:T(8,128)(2,1)S(1)} collective-permute-done((bf16[1,176,512]{2,1,0:T(8,128)(2,1)S(1)}, bf16[1,176,512]{2,1,0:T(8,128)(2,1)S(1)}, u32[]{:S(2)}, u32[]{:S(2)}) %collective-permute-start.11) | collective-permute-done | bytes 180256 | tf_op jit(solution)/shard_map/ppermute | solution.py:620
  140.2 1.0 collective-permute-start.3
  141.9 2.8 %collective-permute-done.3.refs_1_ = bf16[1,2,176,128]{3,2,1,0:T(8,128)(2,1)S(1)} collective-permute-done((bf16[1,2,176,128]{3,2,1,0:T(8,128)(2,1)S(1)}, bf16[1,2,176,128]{3,2,1,0:T(8,128)(2,1)S(1)}, u32[]{:S(2)}, u32[]{:S(2)}) %collective-permute-start.3) | collective-permute-done | bytes 90144 | tf_op jit(solution)/shard_map/ppermute | solution.py:712
  145.4 4.2 %attend_longest.1.first_ref = bf16[192,512]{1,0:T(8,128)(2,1)} custom-call(bf16[1,2,176,128]{3,2,1,0:T(8,128)(2,1)} %get-tuple-element.58.refs_0_, bf16[1,2,176,128]{3,2,1,0:T(8,128)(2,1)} %copy-done.20, bf16[1,2,176,128]{3,2,1,0:T(8,128)(2,1)} %copy-done.19, bf16[1,2,176,128]{3,2,1,0:T(8,128)(2,1)} %copy-done.18, bf16[1,2,176,128]{3,2,1,0:T(8,128)(2,1)} %copy-done.17, ...), custom_call_target="tpu_custom_call" | custom-call | flops 1073741824 | bytes 1500000 | tf_op jit(solution)/shard_map/attend_longest/pallas_call | solution.py:434
  149.7 5.7 %collective-permute-done.12.second_ref = bf16[192,512]{1,0:T(8,128)(2,1)S(1)} collective-permute-done((bf16[192,512]{1,0:T(8,128)(2,1)}, bf16[192,512]{1,0:T(8,128)(2,1)S(1)}, u32[]{:S(2)}, u32[]{:S(2)}) %collective-permute-start.12) | collective-permute-done | bytes 196640 | tf_op jit(solution)/shard_map/ppermute | solution.py:620
  156.1 1.8 fold_parts.2.first_ref
  157.9 1.0 collective-permute-start.13
  158.9 1.8 copy-done.1
  160.8 6.8 %attend_heads.4.refs_0_ = bf16[2,192,512]{2,1,0:T(8,128)(2,1)S(1)} custom-call(bf16[32,3,176,128]{3,2,1,0:T(8,128)(2,1)} %all-to-all-done.1.arrived_ref, f32[1,1024]{1,0:T(1,128)S(1)} %select_n.186.bias_ref, bf16[8,176,512]{2,1,0:T(8,128)(2,1)S(1)} %copy-done, bf16[2,1408,512]{2,1,0:T(8,128)(2,1)S(1)} %copy-done.1), custom_call_target="tpu_custom_call" | custom-call | flops 3221225472 | bytes 4000000 | tf_op jit(solution)/shard_map/attend_heads/pallas_call | solution.py:399
  167.6 0.7 copy-done.4
  168.3 4.3 %all-to-all-start.2 = ((bf16[32,1,176,128]{3,2,1,0:T(8,128)(2,1)}), bf16[32,1,176,128]{3,2,1,0:T(8,128)(2,1)S(1)}, u32[]{:S(2)}, u32[]{:S(2)}) async-start(bf16[32,1,176,128]{3,2,1,0:T(8,128)(2,1)} %pack_blocks.3), calls=%async_computation.2 | async-start | bytes 2883584 | tf_op jit(solution)/shard_map/all_to_all | solution.py:672
  172.7 1.8 fold_parts.3
  174.5 2.7 %collective-permute-start.16 = (bf16[192,512]{1,0:T(8,128)(2,1)}, bf16[192,512]{1,0:T(8,128)(2,1)S(1)}, u32[]{:S(2)}, u32[]{:S(2)}) collective-permute-start(bf16[192,512]{1,0:T(8,128)(2,1)} %fold_parts.3), channel_id=1, source_target_pairs={{0,6},{1,7},{2,4},{3,5},{4,2},{5,3},{6,0},{7,1},{8,14},{9,15},{10,... | collective-permute-start | bytes 589832 | tf_op jit(solution)/shard_map/ppermute | solution.py:741
  178.0 1.8 copy-done.2
  179.8 6.8 %attend_heads.6.refs_2_ = bf16[2,192,512]{2,1,0:T(8,128)(2,1)S(1)} custom-call(bf16[32,3,176,128]{3,2,1,0:T(8,128)(2,1)} %all-to-all-done.1.arrived_ref, f32[1,1024]{1,0:T(1,128)S(1)} %select_n.186.bias_ref, bf16[8,176,512]{2,1,0:T(8,128)(2,1)S(1)} %copy-done, bf16[2,1408,512]{2,1,0:T(8,128)(2,1)S(1)} %copy-done.2), custom_call_target="tpu_custom_call" | custom-call | flops 3221225472 | bytes 4000000 | tf_op jit(solution)/shard_map/attend_heads/pallas_call | solution.py:399
  186.6 7.0 %attend_heads.5.refs_1_ = bf16[2,192,512]{2,1,0:T(8,128)(2,1)S(1)} custom-call(bf16[32,3,176,128]{3,2,1,0:T(8,128)(2,1)} %all-to-all-done.1.arrived_ref, f32[1,1024]{1,0:T(1,128)S(1)} %select_n.186.bias_ref, bf16[8,176,512]{2,1,0:T(8,128)(2,1)S(1)} %copy-done, bf16[2,1408,512]{2,1,0:T(8,128)(2,1)S(1)} %copy-done.2), custom_call_target="tpu_custom_call" | custom-call | flops 3221225472 | bytes 4000000 | tf_op jit(solution)/shard_map/attend_heads/pallas_call | solution.py:399
  193.6 0.7 copy-done.6
  194.3 3.7 %collective-permute-done.15 = bf16[192,512]{1,0:T(8,128)(2,1)S(1)} collective-permute-done((bf16[192,512]{1,0:T(8,128)(2,1)}, bf16[192,512]{1,0:T(8,128)(2,1)S(1)}, u32[]{:S(2)}, u32[]{:S(2)}) %collective-permute-start.15) | collective-permute-done | bytes 196640 | tf_op jit(solution)/shard_map/ppermute | solution.py:741
  198.0 1.0 pad_maximum_fusion.own_ref
  199.7 7.5 %all-to-all-done.2.arrived_ref = bf16[32,1,176,128]{3,2,1,0:T(8,128)(2,1)S(1)} async-done(((bf16[32,1,176,128]{3,2,1,0:T(8,128)(2,1)}), bf16[32,1,176,128]{3,2,1,0:T(8,128)(2,1)S(1)}, u32[]{:S(2)}, u32[]{:S(2)}) %all-to-all-start.2) | async-done | bytes 1441824 | tf_op jit(solution)/shard_map/all_to_all | solution.py:672
  207.2 1.8 copy-done.3
  209.0 5.8 %attend_heads.7.refs_3_ = bf16[2,192,512]{2,1,0:T(8,128)(2,1)S(1)} custom-call(bf16[32,1,176,128]{3,2,1,0:T(8,128)(2,1)S(1)} %all-to-all-done.2.arrived_ref, f32[1,1024]{1,0:T(1,128)S(1)} %select_n.186.bias_ref, bf16[8,176,512]{2,1,0:T(8,128)(2,1)S(1)} %copy-done, bf16[2,1408,512]{2,1,0:T(8,128)(2,1)S(1)} %copy-done.3), custom_call_target="tpu_custom_call" | custom-call | flops 3221225472 | bytes 4000000 | tf_op jit(solution)/shard_map/attend_heads/pallas_call | solution.py:399
  214.8 0.7 copy-done.7
  215.5 3.7 %finish_heads.1 = bf16[1408,512]{1,0:T(8,128)(2,1)} custom-call(s32[2]{0:T(128)} %pad_add_fusion.scalars, bf16[4,192,512]{2,1,0:T(8,128)(2,1)} %pad_maximum_fusion.own_ref, bf16[4,192,512]{2,1,0:T(8,128)(2,1)} %collective-permute-done.17.other_ref, bf16[2,192,512]{2,1,0:T(8,128)(2,1)} %copy-done.4, bf16[2,192,512]{2,1,0:T(8,128)(2,1)} %copy-done.6, ...), custom_call_target="tpu_custom_call" | custom-call | tf_op jit(solution)/shard_map/finish_heads/pallas_call | solution.py:502
  (91 shorter events, 9.7 us)
Async XLA Ops:
  1.9 16.9 %copy-start.11 = (s32[32,128]{1,0:T(8,128)S(1)}, s32[32,128]{1,0:T(8,128)}, u32[]{:S(2)}) copy-start(s32[32,128]{1,0:T(8,128)} %param.18) | copy-start | bytes 49156
  11.5 20.5 %all-to-all-start = ((bf16[32,4,1536]{2,1,0:T(4,128)(2,1)}), bf16[32,4,1536]{2,1,0:T(4,128)(2,1)S(1)}, u32[]{:S(2)}, u32[]{:S(2)}) async-start(bf16[32,4,1536]{2,1,0:T(4,128)(2,1)} %merge_pieces.1), calls=%async_computation | async-start | bytes 786432 | tf_op jit(solution)/shard_map/all_to_all | solution.py:672
  32.0 126.9 %all-to-all-start.1 = ((bf16[32,3,176,128]{3,2,1,0:T(8,128)(2,1)}), bf16[32,3,176,128]{3,2,1,0:T(8,128)(2,1)}, u32[]{:S(2)}, u32[]{:S(2)}) async-start(bf16[32,3,176,128]{3,2,1,0:T(8,128)(2,1)} %pack_blocks.2), calls=%async_computation.1 | async-start | bytes 8650752 | tf_op jit(solution)/shard_map/all_to_all | solution.py:672
  35.7 9.0 %copy-start.13 = (bf16[1408,512]{1,0:T(8,128)(2,1)S(1)}, bf16[1408,512]{1,0:T(8,128)(2,1)}, u32[]{:S(2)}) copy-start(bf16[1408,512]{1,0:T(8,128)(2,1)} %param.14) | copy-start | bytes 4325380
  43.3 2.1 copy-start.12
  54.3 6.2 %collective-permute-start = (bf16[4,176,512]{2,1,0:T(8,128)(2,1)S(1)}, bf16[4,176,512]{2,1,0:T(8,128)(2,1)S(1)}, u32[]{:S(2)}, u32[]{:S(2)}) collective-permute-start(bf16[4,176,512]{2,1,0:T(8,128)(2,1)S(1)} %dynamic-slice_bitcast_fusion), channel_id=1, source_target_pairs={{0,1},{1,0},{2,3},{3,2},{4,5},{5,4},{6,7},{7,6},{8,9},{9,8},{10,11... | collective-permute-start | bytes 2162696 | tf_op jit(solution)/shard_map/ppermute | solution.py:620
  61.8 14.2 %collective-permute-start.1 = (bf16[2,176,512]{2,1,0:T(8,128)(2,1)S(1)}, bf16[2,176,512]{2,1,0:T(8,128)(2,1)S(1)}, u32[]{:S(2)}, u32[]{:S(2)}) collective-permute-start(bf16[2,176,512]{2,1,0:T(8,128)(2,1)S(1)} %dynamic-slice_bitcast_fusion.1), channel_id=1, source_target_pairs={{0,2},{1,3},{2,0},{3,1},{4,6},{5,7},{6,4},{7,5},{8,10},{9,11},{10,... | collective-permute-start | bytes 1081352 | tf_op jit(solution)/shard_map/ppermute | solution.py:620
  76.0 19.1 %collective-permute-start.2 = (bf16[1,176,512]{2,1,0:T(8,128)(2,1)S(1)}, bf16[1,176,512]{2,1,0:T(8,128)(2,1)S(1)}, u32[]{:S(2)}, u32[]{:S(2)}) collective-permute-start(bf16[1,176,512]{2,1,0:T(8,128)(2,1)S(1)} %constant_dynamic-slice_fusion.1), channel_id=1, source_target_pairs={{0,4},{1,5},{2,6},{3,7},{4,0},{5,1},{6,2},{7,3},{8,12},{9,13},{10,... | collective-permute-start | bytes 540680 | tf_op jit(solution)/shard_map/ppermute | solution.py:620
  95.2 15.4 %collective-permute-start.10 = (bf16[1,176,512]{2,1,0:T(8,128)(2,1)S(1)}, bf16[1,176,512]{2,1,0:T(8,128)(2,1)S(1)}, u32[]{:S(2)}, u32[]{:S(2)}) collective-permute-start(bf16[1,176,512]{2,1,0:T(8,128)(2,1)S(1)} %dynamic-slice_select_fusion), channel_id=1, source_target_pairs={{0,8},{1,9},{2,10},{3,11},{4,12},{5,13},{6,14},{7,15},{8,0},{9,1},... | collective-permute-start | bytes 540680 | tf_op jit(solution)/shard_map/ppermute | solution.py:620
  97.1 61.8 %copy-start = (bf16[8,176,512]{2,1,0:T(8,128)(2,1)S(1)}, bf16[8,176,512]{2,1,0:T(8,128)(2,1)}, u32[]{:S(2)}) copy-start(bf16[8,176,512]{2,1,0:T(8,128)(2,1)} %project_query.1.query_ref) | copy-start | bytes 4325380
  97.1 19.5 %collective-permute-start.9 = (bf16[1,2,176,128]{3,2,1,0:T(8,128)(2,1)S(1)}, bf16[1,2,176,128]{3,2,1,0:T(8,128)(2,1)S(1)}, u32[]{:S(2)}, u32[]{:S(2)}) collective-permute-start(bf16[1,2,176,128]{3,2,1,0:T(8,128)(2,1)S(1)} %get-tuple-element.96), channel_id=1, source_target_pairs={{0,7},{1,6},{2,5},{3,4},{4,3},{5,2},{6,1},{7,0},{8,15},{9,14},{10,... | collective-permute-start | bytes 270344 | tf_op jit(solution)/shard_map/ppermute | solution.py:712
  97.1 20.4 %collective-permute-start.8 = (bf16[1,2,176,128]{3,2,1,0:T(8,128)(2,1)S(1)}, bf16[1,2,176,128]{3,2,1,0:T(8,128)(2,1)S(1)}, u32[]{:S(2)}, u32[]{:S(2)}) collective-permute-start(bf16[1,2,176,128]{3,2,1,0:T(8,128)(2,1)S(1)} %get-tuple-element.97), channel_id=1, source_target_pairs={{0,3},{1,2},{2,1},{3,0},{4,7},{5,6},{6,5},{7,4},{8,11},{9,10},{10,... | collective-permute-start | bytes 270344 | tf_op jit(solution)/shard_map/ppermute | solution.py:712
  110.6 29.6 %collective-permute-start.11 = (bf16[1,176,512]{2,1,0:T(8,128)(2,1)S(1)}, bf16[1,176,512]{2,1,0:T(8,128)(2,1)S(1)}, u32[]{:S(2)}, u32[]{:S(2)}) collective-permute-start(bf16[1,176,512]{2,1,0:T(8,128)(2,1)S(1)} %broadcast_select_fusion), channel_id=1, source_target_pairs={{0,16},{1,17},{2,18},{3,19},{4,20},{5,21},{6,22},{7,23},{8,24},{9,... | collective-permute-start | bytes 540680 | tf_op jit(solution)/shard_map/ppermute | solution.py:620
  114.8 27.1 %collective-permute-start.7 = (bf16[1,2,176,128]{3,2,1,0:T(8,128)(2,1)S(1)}, bf16[1,2,176,128]{3,2,1,0:T(8,128)(2,1)S(1)}, u32[]{:S(2)}, u32[]{:S(2)}) collective-permute-start(bf16[1,2,176,128]{3,2,1,0:T(8,128)(2,1)S(1)} %get-tuple-element.98), channel_id=1, source_target_pairs={{0,5},{1,4},{2,7},{3,6},{4,1},{5,0},{6,3},{7,2},{8,13},{9,12},{10,... | collective-permute-start | bytes 270344 | tf_op jit(solution)/shard_map/ppermute | solution.py:712
  115.5 26.4 %collective-permute-start.6 = (bf16[1,2,176,128]{3,2,1,0:T(8,128)(2,1)S(1)}, bf16[1,2,176,128]{3,2,1,0:T(8,128)(2,1)S(1)}, u32[]{:S(2)}, u32[]{:S(2)}) collective-permute-start(bf16[1,2,176,128]{3,2,1,0:T(8,128)(2,1)S(1)} %get-tuple-element.99), channel_id=1, source_target_pairs={{0,1},{1,0},{2,3},{3,2},{4,5},{5,4},{6,7},{7,6},{8,9},{9,8},{10,11... | collective-permute-start | bytes 270344 | tf_op jit(solution)/shard_map/ppermute | solution.py:712
  116.6 28.1 %copy-start.14 = (bf16[1,2,176,128]{3,2,1,0:T(8,128)(2,1)}, bf16[1,2,176,128]{3,2,1,0:T(8,128)(2,1)S(1)}, u32[]{:S(2)}) copy-start(bf16[1,2,176,128]{3,2,1,0:T(8,128)(2,1)S(1)} %collective-permute-done.9.refs_7_) | copy-start | bytes 270340
  116.6 25.3 %collective-permute-start.5 = (bf16[1,2,176,128]{3,2,1,0:T(8,128)(2,1)S(1)}, bf16[1,2,176,128]{3,2,1,0:T(8,128)(2,1)S(1)}, u32[]{:S(2)}, u32[]{:S(2)}) collective-permute-start(bf16[1,2,176,128]{3,2,1,0:T(8,128)(2,1)S(1)} %get-tuple-element.100), channel_id=1, source_target_pairs={{0,6},{1,7},{2,4},{3,5},{4,2},{5,3},{6,0},{7,1},{8,14},{9,15},{10,... | collective-permute-start | bytes 270344 | tf_op jit(solution)/shard_map/ppermute | solution.py:712
  117.5 27.2 %copy-start.15 = (bf16[1,2,176,128]{3,2,1,0:T(8,128)(2,1)}, bf16[1,2,176,128]{3,2,1,0:T(8,128)(2,1)S(1)}, u32[]{:S(2)}) copy-start(bf16[1,2,176,128]{3,2,1,0:T(8,128)(2,1)S(1)} %collective-permute-done.8.refs_6_) | copy-start | bytes 270340
  117.5 24.4 %collective-permute-start.4 = (bf16[1,2,176,128]{3,2,1,0:T(8,128)(2,1)S(1)}, bf16[1,2,176,128]{3,2,1,0:T(8,128)(2,1)S(1)}, u32[]{:S(2)}, u32[]{:S(2)}) collective-permute-start(bf16[1,2,176,128]{3,2,1,0:T(8,128)(2,1)S(1)} %get-tuple-element.101), channel_id=1, source_target_pairs={{0,2},{1,3},{2,0},{3,1},{4,6},{5,7},{6,4},{7,5},{8,10},{9,11},{10,... | collective-permute-start | bytes 270344 | tf_op jit(solution)/shard_map/ppermute | solution.py:712
  140.2 4.5 %collective-permute-start.3 = (bf16[1,2,176,128]{3,2,1,0:T(8,128)(2,1)S(1)}, bf16[1,2,176,128]{3,2,1,0:T(8,128)(2,1)S(1)}, u32[]{:S(2)}, u32[]{:S(2)}) collective-permute-start(bf16[1,2,176,128]{3,2,1,0:T(8,128)(2,1)S(1)} %get-tuple-element.102), channel_id=1, source_target_pairs={{0,4},{1,5},{2,6},{3,7},{4,0},{5,1},{6,2},{7,3},{8,12},{9,13},{10,... | collective-permute-start | bytes 270344 | tf_op jit(solution)/shard_map/ppermute | solution.py:712
  141.9 2.9 %copy-start.16 = (bf16[1,2,176,128]{3,2,1,0:T(8,128)(2,1)}, bf16[1,2,176,128]{3,2,1,0:T(8,128)(2,1)S(1)}, u32[]{:S(2)}) copy-start(bf16[1,2,176,128]{3,2,1,0:T(8,128)(2,1)S(1)} %collective-permute-done.7.refs_5_) | copy-start | bytes 270340
  141.9 2.9 %copy-start.17 = (bf16[1,2,176,128]{3,2,1,0:T(8,128)(2,1)}, bf16[1,2,176,128]{3,2,1,0:T(8,128)(2,1)S(1)}, u32[]{:S(2)}) copy-start(bf16[1,2,176,128]{3,2,1,0:T(8,128)(2,1)S(1)} %collective-permute-done.6.refs_4_) | copy-start | bytes 270340
  141.9 2.9 %copy-start.18 = (bf16[1,2,176,128]{3,2,1,0:T(8,128)(2,1)}, bf16[1,2,176,128]{3,2,1,0:T(8,128)(2,1)S(1)}, u32[]{:S(2)}) copy-start(bf16[1,2,176,128]{3,2,1,0:T(8,128)(2,1)S(1)} %collective-permute-done.5.refs_3_) | copy-start | bytes 270340
  141.9 2.9 %copy-start.19 = (bf16[1,2,176,128]{3,2,1,0:T(8,128)(2,1)}, bf16[1,2,176,128]{3,2,1,0:T(8,128)(2,1)S(1)}, u32[]{:S(2)}) copy-start(bf16[1,2,176,128]{3,2,1,0:T(8,128)(2,1)S(1)} %collective-permute-done.4.refs_2_) | copy-start | bytes 270340
  144.7 0.6 copy-start.20
  149.6 5.9 %collective-permute-start.12 = (bf16[192,512]{1,0:T(8,128)(2,1)}, bf16[192,512]{1,0:T(8,128)(2,1)S(1)}, u32[]{:S(2)}, u32[]{:S(2)}) collective-permute-start(bf16[192,512]{1,0:T(8,128)(2,1)} %attend_longest.1.first_ref), channel_id=1, source_target_pairs={{0,8},{1,9},{2,10},{3,11},{4,12},{5,13},{6,14},{7,15},{8,0},{9,1},... | collective-permute-start | bytes 589832 | tf_op jit(solution)/shard_map/ppermute | solution.py:620
  155.5 0.7 copy-start.10
  157.9 10.4 %collective-permute-start.13 = (bf16[192,512]{1,0:T(8,128)(2,1)}, bf16[192,512]{1,0:T(8,128)(2,1)S(1)}, u32[]{:S(2)}, u32[]{:S(2)}) collective-permute-start(bf16[192,512]{1,0:T(8,128)(2,1)} %fold_parts.2.first_ref), channel_id=1, source_target_pairs={{0,16},{1,17},{2,18},{3,19},{4,20},{5,21},{6,22},{7,23},{8,24},{9,... | collective-permute-start | bytes 589832 | tf_op jit(solution)/shard_map/ppermute | solution.py:620
  158.9 1.8 copy-start.1
  167.5 0.8 copy-start.4
  168.3 4.4 %copy-start.9 = (bf16[192,512]{1,0:T(8,128)(2,1)}, bf16[192,512]{1,0:T(8,128)(2,1)S(1)}, u32[]{:S(2)}) copy-start(bf16[192,512]{1,0:T(8,128)(2,1)S(1)} %collective-permute-done.13.second_ref) | copy-start | bytes 589828
  168.3 38.9 %all-to-all-start.2 = ((bf16[32,1,176,128]{3,2,1,0:T(8,128)(2,1)}), bf16[32,1,176,128]{3,2,1,0:T(8,128)(2,1)S(1)}, u32[]{:S(2)}, u32[]{:S(2)}) async-start(bf16[32,1,176,128]{3,2,1,0:T(8,128)(2,1)} %pack_blocks.3), calls=%async_computation.2 | async-start | bytes 2883584 | tf_op jit(solution)/shard_map/all_to_all | solution.py:672
  174.5 19.9 %collective-permute-start.16 = (bf16[192,512]{1,0:T(8,128)(2,1)}, bf16[192,512]{1,0:T(8,128)(2,1)S(1)}, u32[]{:S(2)}, u32[]{:S(2)}) collective-permute-start(bf16[192,512]{1,0:T(8,128)(2,1)} %fold_parts.3), channel_id=1, source_target_pairs={{0,6},{1,7},{2,4},{3,5},{4,2},{5,3},{6,0},{7,1},{8,14},{9,15},{10,... | collective-permute-start | bytes 589832 | tf_op jit(solution)/shard_map/ppermute | solution.py:741
  177.1 20.9 %collective-permute-start.15 = (bf16[192,512]{1,0:T(8,128)(2,1)}, bf16[192,512]{1,0:T(8,128)(2,1)S(1)}, u32[]{:S(2)}, u32[]{:S(2)}) collective-permute-start(bf16[192,512]{1,0:T(8,128)(2,1)} %fold_parts.3), channel_id=1, source_target_pairs={{0,2},{1,3},{2,0},{3,1},{4,6},{5,7},{6,4},{7,5},{8,10},{9,11},{10,... | collective-permute-start | bytes 589832 | tf_op jit(solution)/shard_map/ppermute | solution.py:741
  177.7 20.3 %collective-permute-start.14 = (bf16[192,512]{1,0:T(8,128)(2,1)}, bf16[192,512]{1,0:T(8,128)(2,1)S(1)}, u32[]{:S(2)}, u32[]{:S(2)}) collective-permute-start(bf16[192,512]{1,0:T(8,128)(2,1)} %fold_parts.3), channel_id=1, source_target_pairs={{0,4},{1,5},{2,6},{3,7},{4,0},{5,1},{6,2},{7,3},{8,12},{9,13},{10,... | collective-permute-start | bytes 589832 | tf_op jit(solution)/shard_map/ppermute | solution.py:741
  178.0 1.8 copy-start.2
  186.6 7.0 %copy-start.5 = (bf16[2,192,512]{2,1,0:T(8,128)(2,1)}, bf16[2,192,512]{2,1,0:T(8,128)(2,1)S(1)}, u32[]{:S(2)}) copy-start(bf16[2,192,512]{2,1,0:T(8,128)(2,1)S(1)} %attend_heads.6.refs_2_) | copy-start | bytes 1179652
  186.6 11.5 %copy-start.8 = (bf16[192,512]{1,0:T(8,128)(2,1)S(1)}, bf16[192,512]{1,0:T(8,128)(2,1)}, u32[]{:S(2)}) copy-start(bf16[192,512]{1,0:T(8,128)(2,1)} %fold_parts.3) | copy-start | bytes 589828
  193.6 0.8 copy-start.6
  199.1 16.5 %collective-permute-start.17 = (bf16[4,192,512]{2,1,0:T(8,128)(2,1)}, bf16[4,192,512]{2,1,0:T(8,128)(2,1)}, u32[]{:S(2)}, u32[]{:S(2)}) collective-permute-start(bf16[4,192,512]{2,1,0:T(8,128)(2,1)} %pad_maximum_fusion.own_ref), channel_id=1, source_target_pairs={{0,1},{1,0},{2,3},{3,2},{4,5},{5,4},{6,7},{7,6},{8,9},{9,8},{10,11... | collective-permute-start | bytes 2359304 | tf_op jit(solution)/shard_map/ppermute | solution.py:620
  207.2 1.8 copy-start.3
  214.8 0.8 copy-start.7

commit v3 on v2

--- a/solution.py
+++ b/solution.py
@@ -408,7 +408,7 @@
         out_specs=pl.BlockSpec((2, EXT, rows), lambda i: (0, 0, 0)),
         out_shape=jax.ShapeDtypeStruct((2, EXT, rows), jnp.bfloat16),
         scratch_shapes=[pltpu.VMEM((4, EXT, old + rows), jnp.bfloat16)],
-        compiler_params=pltpu.CompilerParams(vmem_limit_bytes=VMEM // 2),
+        compiler_params=pltpu.CompilerParams(vmem_limit_bytes=VMEM),
         cost_estimate=pl.CostEstimate(
             flops=work * 1024, bytes_accessed=4000000, transcendentals=work
         ),
@@ -478,40 +478,97 @@
     )(first, second)
 
 
+def finish_pairs(longest, stars, parts, out_ref):
+    @pl.when(jnp.logical_not(longest))
+    def _():
+        for i, part in enumerate(parts):
+            out_ref[i * PAIR : (i + 1) * PAIR] = part[0:PAIR]
+
+    @pl.when(longest)
+    def _():
+        for i, part in enumerate(parts):
+            heads, _ = fold_two(part[...].astype(jnp.float32), stars[i]().astype(jnp.float32))
+            out_ref[i * PAIR : (i + 1) * PAIR] = jnp.concatenate(heads, axis=0).astype(jnp.bfloat16)
+
+
 def finish_body(scalars, own_ref, other_ref, *refs):
-    units, out_ref, held = refs[:-2], refs[-2], refs[-1]
-    pairs = held.shape[0]
-    for i in range(pairs):
-        out_ref[i * PAIR : (i + 1) * PAIR] = units[i // 2][i % 2, 0:PAIR]
-
-    @pl.when(scalars[0] == 1)
-    def _():
-        for i in range(pairs):
-            held[i] = units[i // 2][i % 2]
-        for i in range(pairs):
-            pair = scalars[1] ^ i
-            star = own_ref[i] if i < pairs // 2 else other_ref[i - pairs // 2]
-            heads, _ = fold_two(held[pair].astype(jnp.float32), star.astype(jnp.float32))
-            span = pl.ds(pl.multiple_of(pair * PAIR, 16), PAIR)
-            out_ref[span] = jnp.concatenate(heads, axis=0).astype(jnp.bfloat16)
+    parts = [ref.at[g] for ref in refs[:-1] for g in range(2)]
+    half = own_ref.shape[0]
+
+    def star(i):
+        place = scalars[1] ^ i
+        return jnp.where(place < half, own_ref[place % half], other_ref[place % half])
+
+    stars = [functools.partial(star, i) for i in range(len(parts))]
+    finish_pairs(scalars[0] == 1, stars, parts, refs[-1])
 
 
 def finish(scalars, own, other, units):
-    pairs = 2 * own.shape[0]
-    rows = own.shape[2]
+    half, _, rows = own.shape
     return pl.pallas_call(
         finish_body,
         grid_spec=pltpu.PrefetchScalarGridSpec(
             num_scalar_prefetch=1,
             grid=(1,),
             in_specs=[pl.BlockSpec(x.shape, lambda i, s: (0, 0, 0)) for x in [own, other] + units],
-            out_specs=pl.BlockSpec((pairs * PAIR, rows), lambda i, s: (0, 0)),
-            scratch_shapes=[pltpu.VMEM((pairs, EXT, rows), jnp.bfloat16)],
-        ),
-        out_shape=jax.ShapeDtypeStruct((pairs * PAIR, rows), jnp.bfloat16),
+            out_specs=pl.BlockSpec((2 * len(units) * PAIR, rows), lambda i, s: (0, 0)),
+        ),
+        out_shape=jax.ShapeDtypeStruct((2 * half * PAIR, rows), jnp.bfloat16),
         compiler_params=pltpu.CompilerParams(vmem_limit_bytes=VMEM),
         name="finish_heads",
     )(scalars, own, other, *units)
+
+
+def last_body(scalars, arrived, bias, query, cache, *refs, rows, unit, half):
+    own, other, out_ref, kv, part = refs[0:2], refs[2:4], *refs[5:]
+    attend_body(arrived, bias, query, cache, part, kv, own_rows=rows)
+
+    def star(g):
+        return jnp.where((scalars[1] ^ (2 * unit + g)) < half, own[g][0], other[g][0])
+
+    stars = [functools.partial(star, g) for g in range(2)]
+    finish_pairs(scalars[0] == 1, stars, [part.at[0], part.at[1]], out_ref)
+
+
+def attend_last(scalars, arrived, bias, queries, new_cache, own, other, output, unit):
+    rows = queries.shape[2]
+    old = bias.shape[1]
+    work = 4 * rows * (old + rows)
+    half = own.shape[0]
+
+    def star_spec(g):
+        return pl.BlockSpec((1, EXT, rows), lambda i, s: ((s[1] ^ (2 * unit + g)) % half, 0, 0))
+
+    return pl.pallas_call(
+        functools.partial(last_body, rows=rows, unit=unit, half=half),
+        grid_spec=pltpu.PrefetchScalarGridSpec(
+            num_scalar_prefetch=1,
+            grid=(1,),
+            in_specs=[
+                pl.BlockSpec((arrived.shape[0], 1, PAIR, LANES), lambda i, s: (0, 0, 0, 0)),
+                pl.BlockSpec((1, old), lambda i, s: (0, 0)),
+                pl.BlockSpec((2, PAIR, rows), lambda i, s: (unit, 0, 0)),
+                pl.BlockSpec((2, 2 * PAIR, rows), lambda i, s: (0, unit, 0)),
+                star_spec(0),
+                star_spec(1),
+                star_spec(0),
+                star_spec(1),
+                pl.BlockSpec(memory_space=pl.ANY),
+            ],
+            out_specs=pl.BlockSpec((2 * PAIR, rows), lambda i, s: (unit, 0)),
+            scratch_shapes=[
+                pltpu.VMEM((4, EXT, old + rows), jnp.bfloat16),
+                pltpu.VMEM((2, EXT, rows), jnp.bfloat16),
+            ],
+        ),
+        out_shape=jax.ShapeDtypeStruct(output.shape, jnp.bfloat16),
+        input_output_aliases={9: 0},
+        compiler_params=pltpu.CompilerParams(vmem_limit_bytes=VMEM),
+        cost_estimate=pl.CostEstimate(
+            flops=work * 1024, bytes_accessed=5000000, transcendentals=work
+        ),
+        name="attend_last",
+    )(scalars, arrived, bias, queries, new_cache, own, own, other, other, output)
 
 
 def merge_body(slots, vision_ref, gain_ref, weight_ref, out_ref, total, *, rows_here, width):
@@ -519,7 +576,7 @@
     floats = vision_ref[0].astype(jnp.float32)
     average = jnp.sum(floats, axis=1, keepdims=True) / D
     spread = jnp.sum(floats * floats, axis=1, keepdims=True) / D - average * average
-    normed = ((floats - average) * lax.rsqrt(spread + 1e-06) * gain_ref[...]).astype(jnp.bfloat16)
+    normed = ((floats - average) * lax.rsqrt(spread + 1e-06) * gain_ref[...].reshape(1, width)).astype(jnp.bfloat16)
     product = jnp.dot(normed, weight_ref[0], preferred_element_type=jnp.float32)
 
     @pl.when(step == 0)
@@ -564,7 +621,7 @@
             grid=(parts,),
             in_specs=[
                 pl.BlockSpec((1, groups, width), lambda i, s: (i, 0, 0)),
-                pl.BlockSpec((1, width), lambda i, s: (0, 0)),
+                pl.BlockSpec((width,), lambda i, s: (0,)),
                 pl.BlockSpec((1, width, width), lambda i, s: (i, 0, 0)),
             ],
             out_specs=pl.BlockSpec((devices, piece_rows, width + LANES), lambda i, s: (0, 0, 0)),
@@ -578,7 +635,7 @@
             transcendentals=0,
         ),
         name="merge_pieces",
-    )(image_slot, jnp.transpose(vision, (0, 2, 1)), ln_gain.reshape(1, width), merge_proj)
+    )(image_slot, jnp.transpose(vision, (0, 2, 1)), ln_gain, merge_proj)
 
 
 def place_and_norm(arrived, text, rms_gain):
@@ -744,11 +801,11 @@
     own, results = tie((own, results))
     own = jnp.stack(own)
     other = swap(own, 0)
-    while len(results) < units:
-        attend_next(own)
-    other, results = tie((other, results))
     scalars = jnp.stack([(here == longest).astype(jnp.int32), pair.astype(jnp.int32)])
-    return (finish(scalars, own, other, results), new_cache)
+    output = finish(scalars, own, other, results)
+    output, came[1] = tie((output, came[1]))
+    output = attend_last(scalars, came[1], bias, queries, new_cache, own, other, output, head)
+    return (output, new_cache)
 
 
 def spreads(mesh):

time: 221 us -> 217 us (0.982)
  local copies, waits for them, and re-layouts: 14.2 us -> 7.91 us
  Pallas kernels: 84.3 us -> 90 us
    pallas_call x0 -> x1, Pallas kernels: none -> 8.68 us  [attend_last(): pl.pallas_call(functools.partial(last_body, rows=rows, unit=unit, half=ha...]
    unnamed x42 -> x34, local copies, waits for them, and re-layouts: 9 us -> 3.33 us
    all_to_all x3, waiting for transfers between devices: 10.4 us -> 5.08 us  [exchange(): return lax.all_to_all(x, 'blk', split_axis=0, concat_axis=0, tiled=True)]
    ppermute x8, waiting for transfers between devices: 43.4 us -> 47.6 us  [swap(): return lax.ppermute(x, 'blk', [(i, i ^ 1 << bit) for i in range(size)])]
    ppermute x8, starting transfers between devices: 18.8 us -> 15.4 us  [swap(): return lax.ppermute(x, 'blk', [(i, i ^ 1 << bit) for i in range(size)])]
    pallas_call x4 -> x3, Pallas kernels: 26.3 us -> 23.4 us  [attend_unit(): pl.pallas_call(functools.partial(attend_body, own_rows=rows), grid=(1,),...]
    ppermute x7, starting transfers between devices: 5.79 us -> 8.19 us  [spread_shards(): lax.ppermute(star_kv[i:i + 1], 'blk', [(d, d ^ away) for d in range(devic...]
  transfers between devices with their start and end apart: 21 -> 21, of which waited for: 8 -> 11; matrix products, arithmetic and copies ran while one was open for 6% -> 6% of each run, Pallas kernels for 32% -> 33%
where the time goes in v3:
time: 217 us; the launch traced here: 216 us
  Pallas kernels  90 us (41%)
  waiting for transfers between devices  59.9 us (28%)
  starting transfers between devices  43.2 us (20%)
  local copies, waits for them, and re-layouts  7.91 us (4%)
  other arithmetic  7.72 us (4%)
  between operations  6.35 us (3%)
    ppermute x8, waiting for transfers between devices, swap(): return lax.ppermute(x, 'blk', [(i, i ^ 1 << bit) for i in range(size)])  47.6 us
    pallas_call x3, Pallas kernels, attend_unit(): pl.pallas_call(functools.partial(attend_body, own_rows=rows), grid=(1,),...  23.4 us
    all_to_all x3, starting transfers between devices, exchange(): return lax.all_to_all(x, 'blk', split_axis=0, concat_axis=0, tiled=True)  16.2 us
    ppermute x8, starting transfers between devices, swap(): return lax.ppermute(x, 'blk', [(i, i ^ 1 << bit) for i in range(size)])  15.4 us
    pallas_call x2, Pallas kernels, project(): pl.pallas_call(query_body if query else cache_body, grid=(pairs // 2,), i...  15 us
    pallas_call x2, Pallas kernels, pack_units(): pl.pallas_call(functools.partial(pack_body, slots=slots), grid_spec=pltpu...  15 us
    pallas_call x1, Pallas kernels, merge_rows(): pl.pallas_call(functools.partial(merge_body, rows_here=rows_here, width=w...  9.62 us
    pallas_call x1, Pallas kernels, attend_last(): pl.pallas_call(functools.partial(last_body, rows=rows, unit=unit, half=ha...  8.68 us
  transfers between devices with their start and end apart: 21, of which 11 were waited for; matrix products, arithmetic and copies ran while one was open for 6% of the time, Pallas kernels for 33%

profile of v3, /device:TPU:0, one launch (start us, length us, event | category | flops | bytes accessed | tf_op | source)
XLA Modules:
  0.0 215.7 jit_solution(17020721632654436262)
XLA Ops:
  0.6 9.6 %merge_pieces.1 = bf16[32,4,1536]{2,1,0:T(4,128)(2,1)} custom-call(s32[16]{0:T(128)} %slots.1, bf16[4,64,1408]{2,1,0:T(8,128)(2,1)} %bitcast.42, f32[1408]{0:T(1024)} %gain_ref.1, bf16[4,1408,1408]{2,1,0:T(8,128)(2,1)} %weight_ref.2), custom_call_target="tpu_custom_call" | custom-call | flops 1015021568 | bytes 15859712 | tf_op jit(solution)/shard_map/merge_pieces/pallas_call | solution.py:617
  10.3 7.3 %all-to-all-start = ((bf16[32,4,1536]{2,1,0:T(4,128)(2,1)}), bf16[32,4,1536]{2,1,0:T(4,128)(2,1)S(1)}, u32[]{:S(2)}, u32[]{:S(2)}) async-start(bf16[32,4,1536]{2,1,0:T(4,128)(2,1)} %merge_pieces.1), calls=%async_computation | async-start | bytes 786432 | tf_op jit(solution)/shard_map/all_to_all | solution.py:729
  18.2 9.5 %pack_blocks.2 = bf16[32,3,176,128]{3,2,1,0:T(8,128)(2,1)} custom-call(s32[32]{0:T(128)} %get-tuple-element.82.ids, bf16[2,8,176,2048]{3,2,1,0:T(8,128)(2,1)} %bitcast.27), custom_call_target="tpu_custom_call" | custom-call | bytes 13500000 | tf_op jit(solution)/shard_map/pack_blocks/pallas_call | solution.py:231
  27.8 3.0 %all-to-all-done = bf16[32,4,1536]{2,1,0:T(4,128)(2,1)S(1)} async-done(((bf16[32,4,1536]{2,1,0:T(4,128)(2,1)}), bf16[32,4,1536]{2,1,0:T(4,128)(2,1)S(1)}, u32[]{:S(2)}, u32[]{:S(2)}) %all-to-all-start) | async-done | bytes 393248 | tf_op jit(solution)/shard_map/all_to_all | solution.py:729
  30.7 3.6 %all-to-all-start.1 = ((bf16[32,3,176,128]{3,2,1,0:T(8,128)(2,1)}), bf16[32,3,176,128]{3,2,1,0:T(8,128)(2,1)}, u32[]{:S(2)}, u32[]{:S(2)}) async-start(bf16[32,3,176,128]{3,2,1,0:T(8,128)(2,1)} %pack_blocks.2), calls=%async_computation.1 | async-start | bytes 8650752 | tf_op jit(solution)/shard_map/all_to_all | solution.py:729
  34.4 5.5 %pack_blocks.3 = bf16[32,1,176,128]{3,2,1,0:T(8,128)(2,1)} custom-call(s32[32]{0:T(128)} %get-tuple-element.82.ids, bf16[2,8,176,2048]{3,2,1,0:T(8,128)(2,1)} %bitcast.28), custom_call_target="tpu_custom_call" | custom-call | bytes 4500000 | tf_op jit(solution)/shard_map/pack_blocks/pallas_call | solution.py:231
  41.3 0.8 pad_maximum_fusion.1
  42.2 0.7 multiply_reduce_fusion
  43.5 0.7 fusion
  44.2 1.5 fusion.2.normed_ref
  45.7 6.2 %project_query.1.query_ref.query = bf16[8,176,512]{2,1,0:T(8,128)(2,1)} custom-call(bf16[1408,512]{1,0:T(8,128)(2,1)} %fusion.2.normed_ref, bf16[3,1408,1408]{2,1,0:T(8,128)(2,1)} %value_ref.1, f32[88,512]{1,0:T(8,128)} %get-tuple-element.101.cos_ref, f32[88,512]{1,0:T(8,128)} %get-tuple-element.102.sin_ref), custom_call_target="tpu_custom_call" | custom-call | flops 2030043136 | bytes 5947392 | tf_op jit(solution)/shard_map/project_query/pallas_call | solution.py:319
  51.9 1.3 dynamic-slice_bitcast_fusion
  59.0 1.8 collective-permute-start.1
  60.7 8.8 %project_cache.1.own_ref.cache = bf16[2,1408,512]{2,1,0:T(8,128)(2,1)} custom-call(bf16[1408,512]{1,0:T(8,128)(2,1)} %fusion.2.normed_ref, bf16[3,1408,1408]{2,1,0:T(8,128)(2,1)} %value_ref.1, bf16[3,1408,1408]{2,1,0:T(8,128)(2,1)} %value_ref.1, f32[88,512]{1,0:T(8,128)} %get-tuple-element.101.cos_ref, f32[88,512]{1,0:T(8,128)} %get-tuple-element.102.sin_ref), custom_call_target="tpu_custom_call" | custom-call | flops 4060086272 | bytes 11894784 | tf_op jit(solution)/shard_map/project_cache/pallas_call | solution.py:319
  69.6 4.2 %collective-permute-done.1 = bf16[2,176,512]{2,1,0:T(8,128)(2,1)S(1)} collective-permute-done((bf16[2,176,512]{2,1,0:T(8,128)(2,1)S(1)}, bf16[2,176,512]{2,1,0:T(8,128)(2,1)S(1)}, u32[]{:S(2)}, u32[]{:S(2)}) %collective-permute-start.1) | collective-permute-done | bytes 360480 | tf_op jit(solution)/shard_map/ppermute | solution.py:677
  73.8 8.2 %collective-permute-start.2 = (bf16[1,176,512]{2,1,0:T(8,128)(2,1)S(1)}, bf16[1,176,512]{2,1,0:T(8,128)(2,1)S(1)}, u32[]{:S(2)}, u32[]{:S(2)}) collective-permute-start(bf16[1,176,512]{2,1,0:T(8,128)(2,1)S(1)} %constant_dynamic-slice_fusion.1), channel_id=1, source_target_pairs={{0,4},{1,5},{2,6},{3,7},{4,0},{5,1},{6,2},{7,3},{8,12},{9,13},{10,... | collective-permute-start | bytes 540680 | tf_op jit(solution)/shard_map/ppermute | solution.py:677
  82.7 6.7 %pack_longest.1 = bf16[8,2,176,128]{3,2,1,0:T(8,128)(2,1)} custom-call(s32[5]{0:T(128)} %pad_add_fusion.1.ids, bf16[2,8,176,2048]{3,2,1,0:T(8,128)(2,1)} %bitcast.29, bf16[2,8,176,2048]{3,2,1,0:T(8,128)(2,1)} %bitcast.30, bf16[2,8,176,2048]{3,2,1,0:T(8,128)(2,1)} %bitcast.31, bf16[2,8,176,2048]{3,2,1,0:T(8,128)(2,1)} %bitcast.32, ...), custom_call_target="tpu_custom_call" | custom-call | bytes 4000000 | tf_op jit(solution)/shard_map/pack_longest/pallas_call | solution.py:264
  89.5 1.9 fusion.19
  91.4 3.6 %collective-permute-start.8 = (bf16[1,2,176,128]{3,2,1,0:T(8,128)(2,1)S(1)}, bf16[1,2,176,128]{3,2,1,0:T(8,128)(2,1)S(1)}, u32[]{:S(2)}, u32[]{:S(2)}) collective-permute-start(bf16[1,2,176,128]{3,2,1,0:T(8,128)(2,1)S(1)} %get-tuple-element.89), channel_id=1, source_target_pairs={{0,3},{1,2},{2,1},{3,0},{4,7},{5,6},{6,5},{7,4},{8,11},{9,10},{10,... | collective-permute-start | bytes 270344 | tf_op jit(solution)/shard_map/ppermute | solution.py:769
  95.0 14.3 %collective-permute-done.10 = bf16[1,176,512]{2,1,0:T(8,128)(2,1)S(1)} collective-permute-done((bf16[1,176,512]{2,1,0:T(8,128)(2,1)S(1)}, bf16[1,176,512]{2,1,0:T(8,128)(2,1)S(1)}, u32[]{:S(2)}, u32[]{:S(2)}) %collective-permute-start.10) | collective-permute-done | bytes 180256 | tf_op jit(solution)/shard_map/ppermute | solution.py:677
  109.4 4.1 %collective-permute-start.11 = (bf16[1,176,512]{2,1,0:T(8,128)(2,1)S(1)}, bf16[1,176,512]{2,1,0:T(8,128)(2,1)S(1)}, u32[]{:S(2)}, u32[]{:S(2)}) collective-permute-start(bf16[1,176,512]{2,1,0:T(8,128)(2,1)S(1)} %broadcast_select_fusion), channel_id=1, source_target_pairs={{0,16},{1,17},{2,18},{3,19},{4,20},{5,21},{6,22},{7,23},{8,24},{9,... | collective-permute-start | bytes 540680 | tf_op jit(solution)/shard_map/ppermute | solution.py:677
  114.1 1.2 collective-permute-start.6
  115.3 0.9 collective-permute-start.5
  116.2 0.9 collective-permute-start.4
  117.1 21.8 %collective-permute-done.11 = bf16[1,176,512]{2,1,0:T(8,128)(2,1)S(1)} collective-permute-done((bf16[1,176,512]{2,1,0:T(8,128)(2,1)S(1)}, bf16[1,176,512]{2,1,0:T(8,128)(2,1)S(1)}, u32[]{:S(2)}, u32[]{:S(2)}) %collective-permute-start.11) | collective-permute-done | bytes 180256 | tf_op jit(solution)/shard_map/ppermute | solution.py:677
  138.9 1.0 collective-permute-start.3
  139.9 0.7 broadcast_select_fusion.1.refs_8_
  140.6 2.8 %collective-permute-done.3.refs_1_ = bf16[1,2,176,128]{3,2,1,0:T(8,128)(2,1)S(1)} collective-permute-done((bf16[1,2,176,128]{3,2,1,0:T(8,128)(2,1)S(1)}, bf16[1,2,176,128]{3,2,1,0:T(8,128)(2,1)S(1)}, u32[]{:S(2)}, u32[]{:S(2)}) %collective-permute-start.3) | collective-permute-done | bytes 90144 | tf_op jit(solution)/shard_map/ppermute | solution.py:769
  144.1 4.2 %attend_longest.1.first_ref = bf16[192,512]{1,0:T(8,128)(2,1)} custom-call(bf16[1,2,176,128]{3,2,1,0:T(8,128)(2,1)} %get-tuple-element.54.refs_0_, bf16[1,2,176,128]{3,2,1,0:T(8,128)(2,1)} %copy-done.16, bf16[1,2,176,128]{3,2,1,0:T(8,128)(2,1)} %copy-done.15, bf16[1,2,176,128]{3,2,1,0:T(8,128)(2,1)} %copy-done.14, bf16[1,2,176,128]{3,2,1,0:T(8,128)(2,1)} %copy-done.13, ...), custom_call_target="tpu_custom_call" | custom-call | flops 1073741824 | bytes 1500000 | tf_op jit(solution)/shard_map/attend_longest/pallas_call | solution.py:434
  148.3 0.7 select_n.186.bias_ref.bias
  149.0 5.1 %collective-permute-done.12.second_ref = bf16[192,512]{1,0:T(8,128)(2,1)S(1)} collective-permute-done((bf16[192,512]{1,0:T(8,128)(2,1)}, bf16[192,512]{1,0:T(8,128)(2,1)S(1)}, u32[]{:S(2)}, u32[]{:S(2)}) %collective-permute-start.12) | collective-permute-done | bytes 196640 | tf_op jit(solution)/shard_map/ppermute | solution.py:677
  154.1 0.7 copy-done.6
  154.8 1.8 fold_parts.2.first_ref
  156.6 1.0 collective-permute-start.13
  157.7 7.8 %attend_heads.3.refs_0_ = bf16[2,192,512]{2,1,0:T(8,128)(2,1)} custom-call(bf16[32,3,176,128]{3,2,1,0:T(8,128)(2,1)} %all-to-all-done.1.arrived_ref, f32[1,1024]{1,0:T(1,128)} %select_n.186.bias_ref.bias, bf16[8,176,512]{2,1,0:T(8,128)(2,1)} %project_query.1.query_ref.query, bf16[2,1408,512]{2,1,0:T(8,128)(2,1)} %project_cache.1.own_ref.cache), custom_call_target="tpu_custom_call" | custom-call | flops 3221225472 | bytes 4000000 | tf_op jit(solution)/shard_map/attend_heads/pallas_call | solution.py:399
  166.1 5.3 %all-to-all-start.2 = ((bf16[32,1,176,128]{3,2,1,0:T(8,128)(2,1)}), bf16[32,1,176,128]{3,2,1,0:T(8,128)(2,1)S(1)}, u32[]{:S(2)}, u32[]{:S(2)}) async-start(bf16[32,1,176,128]{3,2,1,0:T(8,128)(2,1)} %pack_blocks.3), calls=%async_computation.2 | async-start | bytes 2883584 | tf_op jit(solution)/shard_map/all_to_all | solution.py:729
  171.4 1.8 fold_parts.3
  173.2 2.5 %collective-permute-start.16 = (bf16[192,512]{1,0:T(8,128)(2,1)}, bf16[192,512]{1,0:T(8,128)(2,1)S(1)}, u32[]{:S(2)}, u32[]{:S(2)}) collective-permute-start(bf16[192,512]{1,0:T(8,128)(2,1)} %fold_parts.3), channel_id=1, source_target_pairs={{0,6},{1,7},{2,4},{3,5},{4,2},{5,3},{6,0},{7,1},{8,14},{9,15},{10,... | collective-permute-start | bytes 589832 | tf_op jit(solution)/shard_map/ppermute | solution.py:798
  176.7 7.8 %attend_heads.5.refs_2_ = bf16[2,192,512]{2,1,0:T(8,128)(2,1)} custom-call(bf16[32,3,176,128]{3,2,1,0:T(8,128)(2,1)} %all-to-all-done.1.arrived_ref, f32[1,1024]{1,0:T(1,128)} %select_n.186.bias_ref.bias, bf16[8,176,512]{2,1,0:T(8,128)(2,1)} %project_query.1.query_ref.query, bf16[2,1408,512]{2,1,0:T(8,128)(2,1)} %project_cache.1.own_ref.cache), custom_call_target="tpu_custom_call" | custom-call | flops 3221225472 | bytes 4000000 | tf_op jit(solution)/shard_map/attend_heads/pallas_call | solution.py:399
  184.5 7.8 %attend_heads.4.refs_1_ = bf16[2,192,512]{2,1,0:T(8,128)(2,1)} custom-call(bf16[32,3,176,128]{3,2,1,0:T(8,128)(2,1)} %all-to-all-done.1.arrived_ref, f32[1,1024]{1,0:T(1,128)} %select_n.186.bias_ref.bias, bf16[8,176,512]{2,1,0:T(8,128)(2,1)} %project_query.1.query_ref.query, bf16[2,1408,512]{2,1,0:T(8,128)(2,1)} %project_cache.1.own_ref.cache), custom_call_target="tpu_custom_call" | custom-call | flops 3221225472 | bytes 4000000 | tf_op jit(solution)/shard_map/attend_heads/pallas_call | solution.py:399
  192.6 4.1 %collective-permute-done.15 = bf16[192,512]{1,0:T(8,128)(2,1)S(1)} collective-permute-done((bf16[192,512]{1,0:T(8,128)(2,1)}, bf16[192,512]{1,0:T(8,128)(2,1)S(1)}, u32[]{:S(2)}, u32[]{:S(2)}) %collective-permute-start.15) | collective-permute-done | bytes 196640 | tf_op jit(solution)/shard_map/ppermute | solution.py:798
  197.0 0.7 pad_add_fusion.scalars
  197.7 1.5 collective-permute-done.17.other_ref.refs_2_.refs_3_
  199.3 0.9 copy-done.3
  200.1 3.7 %finish_heads.1.refs_4_ = bf16[1408,512]{1,0:T(8,128)(2,1)} custom-call(s32[2]{0:T(128)} %pad_add_fusion.scalars, bf16[4,192,512]{2,1,0:T(8,128)(2,1)} %copy-done.1, bf16[4,192,512]{2,1,0:T(8,128)(2,1)} %copy-done.3, bf16[2,192,512]{2,1,0:T(8,128)(2,1)} %attend_heads.3.refs_0_, bf16[2,192,512]{2,1,0:T(8,128)(2,1)} %attend_heads.4.refs_1_, ...), custom_call_target="tpu_custom_call" | custom-call | tf_op jit(solution)/shard_map/finish_heads/pallas_call | solution.py:508
  203.8 2.1 all-to-all-done.2.arrived
  205.9 1.1 copy-done.2
  207.0 8.7 %attend_last.1 = bf16[1408,512]{1,0:T(8,128)(2,1)} custom-call(s32[2]{0:T(128)} %pad_add_fusion.scalars, bf16[32,1,176,128]{3,2,1,0:T(8,128)(2,1)} %copy-done.2, f32[1,1024]{1,0:T(1,128)} %select_n.186.bias_ref.bias, bf16[8,176,512]{2,1,0:T(8,128)(2,1)} %project_query.1.query_ref.query, ...), custom_call_target="tpu_custom_call", output_to_operand_aliasing={{}: (9, {})} | custom-call | flops 3221225472 | bytes 5000000 | tf_op jit(solution)/shard_map/attend_last/pallas_call | solution.py:542
  (82 shorter events, 7.6 us)
Async XLA Ops:
  0.6 16.9 %copy-start.7 = (s32[32,128]{1,0:T(8,128)S(1)}, s32[32,128]{1,0:T(8,128)}, u32[]{:S(2)}) copy-start(s32[32,128]{1,0:T(8,128)} %param.18) | copy-start | bytes 49156
  10.3 20.5 %all-to-all-start = ((bf16[32,4,1536]{2,1,0:T(4,128)(2,1)}), bf16[32,4,1536]{2,1,0:T(4,128)(2,1)S(1)}, u32[]{:S(2)}, u32[]{:S(2)}) async-start(bf16[32,4,1536]{2,1,0:T(4,128)(2,1)} %merge_pieces.1), calls=%async_computation | async-start | bytes 786432 | tf_op jit(solution)/shard_map/all_to_all | solution.py:729
  30.7 126.9 %all-to-all-start.1 = ((bf16[32,3,176,128]{3,2,1,0:T(8,128)(2,1)}), bf16[32,3,176,128]{3,2,1,0:T(8,128)(2,1)}, u32[]{:S(2)}, u32[]{:S(2)}) async-start(bf16[32,3,176,128]{3,2,1,0:T(8,128)(2,1)} %pack_blocks.2), calls=%async_computation.1 | async-start | bytes 8650752 | tf_op jit(solution)/shard_map/all_to_all | solution.py:729
  39.9 3.6 %copy-start.9 = (bf16[1408,512]{1,0:T(8,128)(2,1)S(1)}, bf16[1408,512]{1,0:T(8,128)(2,1)}, u32[]{:S(2)}) copy-start(bf16[1408,512]{1,0:T(8,128)(2,1)} %param.14) | copy-start | bytes 4325380
  43.4 0.7 copy-start.8
  51.9 6.9 %copy-start = (bf16[8,176,512]{2,1,0:T(8,128)(2,1)S(1)}, bf16[8,176,512]{2,1,0:T(8,128)(2,1)}, u32[]{:S(2)}) copy-start(bf16[8,176,512]{2,1,0:T(8,128)(2,1)} %project_query.1.query_ref.query) | copy-start | bytes 4325380
  53.2 5.7 %collective-permute-start = (bf16[4,176,512]{2,1,0:T(8,128)(2,1)S(1)}, bf16[4,176,512]{2,1,0:T(8,128)(2,1)S(1)}, u32[]{:S(2)}, u32[]{:S(2)}) collective-permute-start(bf16[4,176,512]{2,1,0:T(8,128)(2,1)S(1)} %dynamic-slice_bitcast_fusion), channel_id=1, source_target_pairs={{0,1},{1,0},{2,3},{3,2},{4,5},{5,4},{6,7},{7,6},{8,9},{9,8},{10,11... | collective-permute-start | bytes 2162696 | tf_op jit(solution)/shard_map/ppermute | solution.py:677
  59.0 14.7 %collective-permute-start.1 = (bf16[2,176,512]{2,1,0:T(8,128)(2,1)S(1)}, bf16[2,176,512]{2,1,0:T(8,128)(2,1)S(1)}, u32[]{:S(2)}, u32[]{:S(2)}) collective-permute-start(bf16[2,176,512]{2,1,0:T(8,128)(2,1)S(1)} %dynamic-slice_bitcast_fusion.1), channel_id=1, source_target_pairs={{0,2},{1,3},{2,0},{3,1},{4,6},{5,7},{6,4},{7,5},{8,10},{9,11},{10,... | collective-permute-start | bytes 1081352 | tf_op jit(solution)/shard_map/ppermute | solution.py:677
  73.8 15.6 %collective-permute-start.2 = (bf16[1,176,512]{2,1,0:T(8,128)(2,1)S(1)}, bf16[1,176,512]{2,1,0:T(8,128)(2,1)S(1)}, u32[]{:S(2)}, u32[]{:S(2)}) collective-permute-start(bf16[1,176,512]{2,1,0:T(8,128)(2,1)S(1)} %constant_dynamic-slice_fusion.1), channel_id=1, source_target_pairs={{0,4},{1,5},{2,6},{3,7},{4,0},{5,1},{6,2},{7,3},{8,12},{9,13},{10,... | collective-permute-start | bytes 540680 | tf_op jit(solution)/shard_map/ppermute | solution.py:677
  89.4 19.9 %collective-permute-start.10 = (bf16[1,176,512]{2,1,0:T(8,128)(2,1)S(1)}, bf16[1,176,512]{2,1,0:T(8,128)(2,1)S(1)}, u32[]{:S(2)}, u32[]{:S(2)}) collective-permute-start(bf16[1,176,512]{2,1,0:T(8,128)(2,1)S(1)} %dynamic-slice_select_fusion), channel_id=1, source_target_pairs={{0,8},{1,9},{2,10},{3,11},{4,12},{5,13},{6,14},{7,15},{8,0},{9,1},... | collective-permute-start | bytes 540680 | tf_op jit(solution)/shard_map/ppermute | solution.py:677
  91.4 23.9 %collective-permute-start.9 = (bf16[1,2,176,128]{3,2,1,0:T(8,128)(2,1)S(1)}, bf16[1,2,176,128]{3,2,1,0:T(8,128)(2,1)S(1)}, u32[]{:S(2)}, u32[]{:S(2)}) collective-permute-start(bf16[1,2,176,128]{3,2,1,0:T(8,128)(2,1)S(1)} %get-tuple-element.88), channel_id=1, source_target_pairs={{0,7},{1,6},{2,5},{3,4},{4,3},{5,2},{6,1},{7,0},{8,15},{9,14},{10,... | collective-permute-start | bytes 270344 | tf_op jit(solution)/shard_map/ppermute | solution.py:769
  91.4 24.8 %collective-permute-start.8 = (bf16[1,2,176,128]{3,2,1,0:T(8,128)(2,1)S(1)}, bf16[1,2,176,128]{3,2,1,0:T(8,128)(2,1)S(1)}, u32[]{:S(2)}, u32[]{:S(2)}) collective-permute-start(bf16[1,2,176,128]{3,2,1,0:T(8,128)(2,1)S(1)} %get-tuple-element.89), channel_id=1, source_target_pairs={{0,3},{1,2},{2,1},{3,0},{4,7},{5,6},{6,5},{7,4},{8,11},{9,10},{10,... | collective-permute-start | bytes 270344 | tf_op jit(solution)/shard_map/ppermute | solution.py:769
  109.4 29.5 %collective-permute-start.11 = (bf16[1,176,512]{2,1,0:T(8,128)(2,1)S(1)}, bf16[1,176,512]{2,1,0:T(8,128)(2,1)S(1)}, u32[]{:S(2)}, u32[]{:S(2)}) collective-permute-start(bf16[1,176,512]{2,1,0:T(8,128)(2,1)S(1)} %broadcast_select_fusion), channel_id=1, source_target_pairs={{0,16},{1,17},{2,18},{3,19},{4,20},{5,21},{6,22},{7,23},{8,24},{9,... | collective-permute-start | bytes 540680 | tf_op jit(solution)/shard_map/ppermute | solution.py:677
  113.5 27.1 %collective-permute-start.7 = (bf16[1,2,176,128]{3,2,1,0:T(8,128)(2,1)S(1)}, bf16[1,2,176,128]{3,2,1,0:T(8,128)(2,1)S(1)}, u32[]{:S(2)}, u32[]{:S(2)}) collective-permute-start(bf16[1,2,176,128]{3,2,1,0:T(8,128)(2,1)S(1)} %get-tuple-element.90), channel_id=1, source_target_pairs={{0,5},{1,4},{2,7},{3,6},{4,1},{5,0},{6,3},{7,2},{8,13},{9,12},{10,... | collective-permute-start | bytes 270344 | tf_op jit(solution)/shard_map/ppermute | solution.py:769
  114.1 26.4 %collective-permute-start.6 = (bf16[1,2,176,128]{3,2,1,0:T(8,128)(2,1)S(1)}, bf16[1,2,176,128]{3,2,1,0:T(8,128)(2,1)S(1)}, u32[]{:S(2)}, u32[]{:S(2)}) collective-permute-start(bf16[1,2,176,128]{3,2,1,0:T(8,128)(2,1)S(1)} %get-tuple-element.91), channel_id=1, source_target_pairs={{0,1},{1,0},{2,3},{3,2},{4,5},{5,4},{6,7},{7,6},{8,9},{9,8},{10,11... | collective-permute-start | bytes 270344 | tf_op jit(solution)/shard_map/ppermute | solution.py:769
  115.3 28.1 %copy-start.10 = (bf16[1,2,176,128]{3,2,1,0:T(8,128)(2,1)}, bf16[1,2,176,128]{3,2,1,0:T(8,128)(2,1)S(1)}, u32[]{:S(2)}) copy-start(bf16[1,2,176,128]{3,2,1,0:T(8,128)(2,1)S(1)} %collective-permute-done.9.refs_7_) | copy-start | bytes 270340
  115.3 25.3 %collective-permute-start.5 = (bf16[1,2,176,128]{3,2,1,0:T(8,128)(2,1)S(1)}, bf16[1,2,176,128]{3,2,1,0:T(8,128)(2,1)S(1)}, u32[]{:S(2)}, u32[]{:S(2)}) collective-permute-start(bf16[1,2,176,128]{3,2,1,0:T(8,128)(2,1)S(1)} %get-tuple-element.92), channel_id=1, source_target_pairs={{0,6},{1,7},{2,4},{3,5},{4,2},{5,3},{6,0},{7,1},{8,14},{9,15},{10,... | collective-permute-start | bytes 270344 | tf_op jit(solution)/shard_map/ppermute | solution.py:769
  116.2 27.2 %copy-start.11 = (bf16[1,2,176,128]{3,2,1,0:T(8,128)(2,1)}, bf16[1,2,176,128]{3,2,1,0:T(8,128)(2,1)S(1)}, u32[]{:S(2)}) copy-start(bf16[1,2,176,128]{3,2,1,0:T(8,128)(2,1)S(1)} %collective-permute-done.8.refs_6_) | copy-start | bytes 270340
  116.2 24.4 %collective-permute-start.4 = (bf16[1,2,176,128]{3,2,1,0:T(8,128)(2,1)S(1)}, bf16[1,2,176,128]{3,2,1,0:T(8,128)(2,1)S(1)}, u32[]{:S(2)}, u32[]{:S(2)}) collective-permute-start(bf16[1,2,176,128]{3,2,1,0:T(8,128)(2,1)S(1)} %get-tuple-element.93), channel_id=1, source_target_pairs={{0,2},{1,3},{2,0},{3,1},{4,6},{5,7},{6,4},{7,5},{8,10},{9,11},{10,... | collective-permute-start | bytes 270344 | tf_op jit(solution)/shard_map/ppermute | solution.py:769
  138.9 4.5 %collective-permute-start.3 = (bf16[1,2,176,128]{3,2,1,0:T(8,128)(2,1)S(1)}, bf16[1,2,176,128]{3,2,1,0:T(8,128)(2,1)S(1)}, u32[]{:S(2)}, u32[]{:S(2)}) collective-permute-start(bf16[1,2,176,128]{3,2,1,0:T(8,128)(2,1)S(1)} %get-tuple-element.94), channel_id=1, source_target_pairs={{0,4},{1,5},{2,6},{3,7},{4,0},{5,1},{6,2},{7,3},{8,12},{9,13},{10,... | collective-permute-start | bytes 270344 | tf_op jit(solution)/shard_map/ppermute | solution.py:769
  140.6 2.9 %copy-start.12 = (bf16[1,2,176,128]{3,2,1,0:T(8,128)(2,1)}, bf16[1,2,176,128]{3,2,1,0:T(8,128)(2,1)S(1)}, u32[]{:S(2)}) copy-start(bf16[1,2,176,128]{3,2,1,0:T(8,128)(2,1)S(1)} %collective-permute-done.7.refs_5_) | copy-start | bytes 270340
  140.6 2.9 %copy-start.13 = (bf16[1,2,176,128]{3,2,1,0:T(8,128)(2,1)}, bf16[1,2,176,128]{3,2,1,0:T(8,128)(2,1)S(1)}, u32[]{:S(2)}) copy-start(bf16[1,2,176,128]{3,2,1,0:T(8,128)(2,1)S(1)} %collective-permute-done.6.refs_4_) | copy-start | bytes 270340
  140.6 2.8 %copy-start.14 = (bf16[1,2,176,128]{3,2,1,0:T(8,128)(2,1)}, bf16[1,2,176,128]{3,2,1,0:T(8,128)(2,1)S(1)}, u32[]{:S(2)}) copy-start(bf16[1,2,176,128]{3,2,1,0:T(8,128)(2,1)S(1)} %collective-permute-done.5.refs_3_) | copy-start | bytes 270340
  140.6 2.8 %copy-start.15 = (bf16[1,2,176,128]{3,2,1,0:T(8,128)(2,1)}, bf16[1,2,176,128]{3,2,1,0:T(8,128)(2,1)S(1)}, u32[]{:S(2)}) copy-start(bf16[1,2,176,128]{3,2,1,0:T(8,128)(2,1)S(1)} %collective-permute-done.4.refs_2_) | copy-start | bytes 270340
  143.4 0.6 copy-start.16
  148.3 5.9 %collective-permute-start.12 = (bf16[192,512]{1,0:T(8,128)(2,1)}, bf16[192,512]{1,0:T(8,128)(2,1)S(1)}, u32[]{:S(2)}, u32[]{:S(2)}) collective-permute-start(bf16[192,512]{1,0:T(8,128)(2,1)} %attend_longest.1.first_ref), channel_id=1, source_target_pairs={{0,8},{1,9},{2,10},{3,11},{4,12},{5,13},{6,14},{7,15},{8,0},{9,1},... | collective-permute-start | bytes 589832 | tf_op jit(solution)/shard_map/ppermute | solution.py:677
  154.1 0.7 copy-start.6
  156.6 9.5 %collective-permute-start.13 = (bf16[192,512]{1,0:T(8,128)(2,1)}, bf16[192,512]{1,0:T(8,128)(2,1)S(1)}, u32[]{:S(2)}, u32[]{:S(2)}) collective-permute-start(bf16[192,512]{1,0:T(8,128)(2,1)} %fold_parts.2.first_ref), channel_id=1, source_target_pairs={{0,16},{1,17},{2,18},{3,19},{4,20},{5,21},{6,22},{7,23},{8,24},{9,... | collective-permute-start | bytes 589832 | tf_op jit(solution)/shard_map/ppermute | solution.py:677
  166.1 5.3 %copy-start.5 = (bf16[192,512]{1,0:T(8,128)(2,1)}, bf16[192,512]{1,0:T(8,128)(2,1)S(1)}, u32[]{:S(2)}) copy-start(bf16[192,512]{1,0:T(8,128)(2,1)S(1)} %collective-permute-done.13.second_ref) | copy-start | bytes 589828
  166.1 39.8 %all-to-all-start.2 = ((bf16[32,1,176,128]{3,2,1,0:T(8,128)(2,1)}), bf16[32,1,176,128]{3,2,1,0:T(8,128)(2,1)S(1)}, u32[]{:S(2)}, u32[]{:S(2)}) async-start(bf16[32,1,176,128]{3,2,1,0:T(8,128)(2,1)} %pack_blocks.3), calls=%async_computation.2 | async-start | bytes 2883584 | tf_op jit(solution)/shard_map/all_to_all | solution.py:729
  173.2 19.4 %collective-permute-start.16 = (bf16[192,512]{1,0:T(8,128)(2,1)}, bf16[192,512]{1,0:T(8,128)(2,1)S(1)}, u32[]{:S(2)}, u32[]{:S(2)}) collective-permute-start(bf16[192,512]{1,0:T(8,128)(2,1)} %fold_parts.3), channel_id=1, source_target_pairs={{0,6},{1,7},{2,4},{3,5},{4,2},{5,3},{6,0},{7,1},{8,14},{9,15},{10,... | collective-permute-start | bytes 589832 | tf_op jit(solution)/shard_map/ppermute | solution.py:798
  175.7 21.1 %collective-permute-start.15 = (bf16[192,512]{1,0:T(8,128)(2,1)}, bf16[192,512]{1,0:T(8,128)(2,1)S(1)}, u32[]{:S(2)}, u32[]{:S(2)}) collective-permute-start(bf16[192,512]{1,0:T(8,128)(2,1)} %fold_parts.3), channel_id=1, source_target_pairs={{0,2},{1,3},{2,0},{3,1},{4,6},{5,7},{6,4},{7,5},{8,10},{9,11},{10,... | collective-permute-start | bytes 589832 | tf_op jit(solution)/shard_map/ppermute | solution.py:798
  176.3 20.5 %collective-permute-start.14 = (bf16[192,512]{1,0:T(8,128)(2,1)}, bf16[192,512]{1,0:T(8,128)(2,1)S(1)}, u32[]{:S(2)}, u32[]{:S(2)}) collective-permute-start(bf16[192,512]{1,0:T(8,128)(2,1)} %fold_parts.3), channel_id=1, source_target_pairs={{0,4},{1,5},{2,6},{3,7},{4,0},{5,1},{6,2},{7,3},{8,12},{9,13},{10,... | collective-permute-start | bytes 589832 | tf_op jit(solution)/shard_map/ppermute | solution.py:798
  184.5 12.3 %copy-start.4 = (bf16[192,512]{1,0:T(8,128)(2,1)S(1)}, bf16[192,512]{1,0:T(8,128)(2,1)}, u32[]{:S(2)}) copy-start(bf16[192,512]{1,0:T(8,128)(2,1)} %fold_parts.3) | copy-start | bytes 589828
  196.9 2.4 %copy-start.1 = (bf16[4,192,512]{2,1,0:T(8,128)(2,1)}, bf16[4,192,512]{2,1,0:T(8,128)(2,1)S(1)}, u32[]{:S(2)}) copy-start(bf16[4,192,512]{2,1,0:T(8,128)(2,1)S(1)} %pad_maximum_fusion.own_ref.refs_0_.refs_1_) | copy-start | bytes 2359300
  196.9 2.4 %collective-permute-start.17 = (bf16[4,192,512]{2,1,0:T(8,128)(2,1)S(1)}, bf16[4,192,512]{2,1,0:T(8,128)(2,1)S(1)}, u32[]{:S(2)}, u32[]{:S(2)}) collective-permute-start(bf16[4,192,512]{2,1,0:T(8,128)(2,1)S(1)} %pad_maximum_fusion.own_ref.refs_0_.refs_1_), channel_id=1, source_target_pairs={{0,1},{1,0},{2,3},{3,2},{4,5},{5,4},{6,7},{7,6},{8,9},{9,8},{10,11... | collective-permute-start | bytes 2359304 | tf_op jit(solution)/shard_map/ppermute | solution.py:677
  199.3 0.9 copy-start.3
  205.9 1.1 copy-start.2
